TPU v7x, 128 devices: a whole 4x4x4 slice. The times are simulated.
128 devices in a mesh: ctx: 16 (over x, z), head: 8 (over y, core).
Axes of the slice: x: 4, y: 4, z: 4, core: 2. Of those that a mesh axis runs over, the one named last changes fastest.
Arguments:
- queries: bfloat16 [8192, 4096], P('ctx', 'head'), may hold values from -6 to 6
- key_states: bfloat16 [8192, 4096], P('ctx', 'head'), may hold values from -6 to 6
- value_states: bfloat16 [8192, 4096], P('ctx', 'head'), may hold values from -6 to 6
- transition_vectors: bfloat16 [8192, 4096], P('ctx', 'head'), may hold values from -6 to 6
- beta_logit: float32 [8192, 32], P('ctx', 'head'), may hold values from -6 to 6
- document_ids: int32 [8192], P('ctx'), may hold values from 0 to 7, as said below
- out_weight: bfloat16 [4096, 4096], P('head'), may hold values from -0.09375 to 0.09375
Outputs:
- layer_out: bfloat16 [8192, 4096], P(('ctx', 'head'))
Inputs may be any that keep to these rules, and one draw needn't show every extreme that they name: `document_ids`: document ids never fall along the sequence; document 0 is the first 4352 tokens; the other documents have 1 or more tokens each and together fill the rest.
All inputs are finite; a program needn't handle non-finite values.
Results may differ from a plain program's by a relative error of at most 0.022.
Values may be sent and summed in bfloat16 or wider, within the bound.
A program may use at most 128 MiB of HBM per device.

v0:
```python
import jax
import jax.numpy as jnp
from jax import lax
from jax.sharding import PartitionSpec as P

epsilon = 1e-06
masked_value = -1e30
highest = lax.Precision.HIGHEST


def shifted(value, axis, steps):
    count = lax.axis_size(axis)
    first, last = (max(0, -steps), min(count, count - steps))
    return lax.ppermute(value, axis, [(source, source + steps) for source in range(first, last)])


def shard_operators(query_block, key_block, vector_block, strength):
    block_rows = key_block.shape[0]
    head_width = key_block.shape[1]
    row_ids = jnp.arange(block_rows)
    strict = row_ids[:, None] > row_ids[None, :]
    causal = row_ids[:, None] >= row_ids[None, :]
    intersections = jnp.dot(vector_block, vector_block.T, precision=highest)
    unit_lower = jnp.where(strict, intersections * strength[None, :], 0.0) + jnp.eye(
        block_rows, dtype=jnp.float32
    )
    key_proj = jnp.where(strict, jnp.dot(vector_block, key_block.T, precision=highest), 0.0)
    solved = lax.linalg.triangular_solve(
        unit_lower,
        jnp.concatenate([key_proj, vector_block], axis=1),
        left_side=True,
        lower=True,
        unit_diagonal=True,
    )
    key_solve = solved[:, :block_rows]
    vector_solve = solved[:, block_rows:]
    weighted = strength[:, None] * vector_block
    keys_end = (key_block - jnp.dot(key_solve.T, weighted, precision=highest)).astype(jnp.bfloat16)
    transfer = jnp.eye(head_width, dtype=jnp.float32) - jnp.dot(
        vector_block.T, strength[:, None] * vector_solve, precision=highest
    )
    query_dots = jnp.where(causal, jnp.dot(query_block, vector_block.T, precision=highest), 0.0)
    scaled_dots = query_dots * strength[None, :]
    intra_scores = jnp.dot(query_block, key_block.T, precision=highest) - jnp.dot(
        scaled_dots, key_solve, precision=highest
    )
    rotated = query_block - jnp.dot(scaled_dots, vector_solve, precision=highest)
    return (intra_scores, keys_end, transfer, rotated)


def on_device(
    queries, key_states, value_states, transition_vectors, beta_logit, document_ids, out_weight
):
    block_rows = queries.shape[0]
    head_count = beta_logit.shape[1]
    head_width = queries.shape[1] // head_count
    score_scale = head_width ** (-0.5)

    def split_heads(flat):
        return jnp.transpose(flat.reshape(block_rows, head_count, head_width), (1, 0, 2))

    query_heads = split_heads(queries).astype(jnp.float32)
    key_heads = split_heads(key_states).astype(jnp.float32)
    value_heads = split_heads(value_states)
    vector_heads = split_heads(transition_vectors).astype(jnp.float32)
    unit_vectors = vector_heads / jnp.sqrt(
        jnp.sum(vector_heads * vector_heads, axis=2, keepdims=True) + epsilon
    )
    strength = 2.0 * jax.nn.sigmoid(beta_logit.T)
    intra_scores, keys_end, transfer, rotated = jax.vmap(shard_operators)(
        query_heads, key_heads, unit_vectors, strength
    )
    row_ids = jnp.arange(block_rows)
    causal = row_ids[:, None] >= row_ids[None, :]
    doc_float = (document_ids + 1).astype(jnp.float32)
    same_doc = doc_float[:, None] == doc_float[None, :]
    own_scores = jnp.where((causal & same_doc)[None], intra_scores * score_scale, masked_value)
    running_max = jnp.max(own_scores, axis=2)
    weights = jnp.exp(own_scores - running_max[..., None])
    running_sum = jnp.sum(weights, axis=2)
    accumulated = jnp.einsum(
        "hqk,hkd->hqd",
        weights.astype(jnp.bfloat16),
        value_heads,
        preferred_element_type=jnp.float32,
    )
    ctx_index = lax.axis_index("ctx")
    ctx_count = lax.axis_size("ctx")
    packed = jnp.stack([keys_end, value_heads])

    def attend(carried, key_pair, transfer_in, key_docs, is_live):
        turned, running_max, running_sum, accumulated = carried
        scores = jnp.einsum(
            "hqd,hkd->hqk",
            turned.astype(jnp.bfloat16),
            key_pair[0],
            preferred_element_type=jnp.float32,
        )
        allowed = (doc_float[:, None] == key_docs[None, :]) & is_live
        scores = jnp.where(allowed[None], scores * score_scale, masked_value)
        new_max = jnp.maximum(running_max, jnp.max(scores, axis=2))
        factor = jnp.exp(running_max - new_max)
        weights = jnp.exp(scores - new_max[..., None])
        running_sum = running_sum * factor + jnp.sum(weights, axis=2)
        accumulated = accumulated * factor[..., None] + jnp.einsum(
            "hqk,hkd->hqd",
            weights.astype(jnp.bfloat16),
            key_pair[1],
            preferred_element_type=jnp.float32,
        )
        turned = jnp.einsum("hqd,hde->hqe", turned, transfer_in, precision=highest)
        return (turned, new_max, running_sum, accumulated)

    def visit(carried, key_pair, transfer_in, key_docs, is_live):
        return attend(carried, key_pair, transfer_in, key_docs, is_live)

    carried = (rotated, running_max, running_sum, accumulated)

    def relay_step(offset, looped):
        key_pair, transfer_in, key_docs, inner = looped
        key_pair = shifted(key_pair, "ctx", 1)
        transfer_in, key_docs = (
            shifted(transfer_in.astype(jnp.bfloat16), "ctx", 1).astype(transfer_in.dtype),
            shifted(key_docs.astype(jnp.bfloat16), "ctx", 1).astype(key_docs.dtype),
        )
        inner = visit(inner, key_pair, transfer_in, key_docs, ctx_index - offset >= 0)
        return (key_pair, transfer_in, key_docs, inner)

    looped = lax.fori_loop(1, ctx_count, relay_step, (packed, transfer, doc_float, carried))
    carried = looped[3]
    attended = (carried[3] / carried[2][..., None]).astype(jnp.bfloat16)
    token_rows = jnp.transpose(attended, (1, 0, 2)).reshape(block_rows, head_count * head_width)
    return lax.psum_scatter(
        jnp.dot(token_rows, out_weight, preferred_element_type=jnp.float32).astype(jnp.bfloat16),
        "head",
        scatter_dimension=0,
        tiled=True,
    )


def solution(mesh):
    return jax.shard_map(
        on_device,
        mesh=mesh,
        in_specs=(
            P("ctx", "head"),
            P("ctx", "head"),
            P("ctx", "head"),
            P("ctx", "head"),
            P("ctx", "head"),
            P("ctx"),
            P("head", None),
        ),
        out_specs=P(("ctx", "head"), None),
        check_vma=False,
    )
```

profile of v0, /device:TPU:5, one launch (start us, length us, event | category | flops | bytes accessed | tf_op | source)
XLA Modules:
  0.0 800.1 jit_solution(8162292102818051516)
XLA Ops:
  13.7 3.9 convolution_select_fusion
  17.6 6.1 select_add_fusion
  23.7 14.8 %while.27 = (s32[]{:T(128)}, f32[4,512,512]{2,1,0:T(8,128)}, s32[4,2]{0,1:T(2,128)S(1)}, f32[4,4,128,128]{3,2,0,1:T(8,128)}, s32[]{:T(128)}) while((s32[]{:T(128)}, f32[4,512,512]{2,1,0:T(8,128)}, s32[4,2]{0,1:T(2,128)S(1)}, f32[4,4,128,128]{3,2,0,1:T(8,128)}, s32[]{:T(128)}) %tuple.51), condition=%wide.while_cond, body=%wide.while_body.sunk | while | flops 2 | bytes 525421 | solution.py:28
  24.3 3.1 bitcast_dynamic-update-slice_fusion.2
  28.0 3.1 bitcast_dynamic-update-slice_fusion.2
  31.7 3.1 bitcast_dynamic-update-slice_fusion.2
  35.5 3.0 bitcast_dynamic-update-slice_fusion.2
  38.5 158.2 %custom-call.3 = f32[4,4,128,128]{2,3,1,0:T(8,128)S(1)} custom-call(f32[4,4,128,128]{3,2,1,0:T(8,128)} %bitcast.107), custom_call_target="InvertDiagBlocksLowerTriangular" | custom-call | tf_op jit(solution)/shard_map/vmap()/triangular_solve | solution.py:28
  196.7 2.6 fusion.59
  202.8 2.9 fusion.45
  207.0 4.1 fusion.48
  212.4 2.7 pad_maximum_fusion
  218.9 10.0 %fusion.65 = bf16[1,4,512,128]{3,2,1,0:T(8,128)(2,1)} fusion(f32[4,512,640]{2,1,0:T(8,128)} %pad_maximum_fusion, f32[4,512,128]{2,1,0:T(8,128)S(1)} %bitcast_divide_fusion, bf16[512,4,128]{2,0,1:T(8,128)(2,1)S(1)} %copy.23, f32[4,512]{1,0:T(4,128)S(1)} %multiply_bitcast_fusion), kind=kOutput, calls=%fused_computation.72 | convolution fusion | flops 1611661312 | bytes 6299648 | tf_op jit(solution)/shard_map/vmap()/dot_general | solution.py:38
  232.3 11.0 %fusion.17 = f32[4,512,512]{1,2,0:T(8,128)} fusion(f32[4,512,640]{2,1,0:T(8,128)} %pad_maximum_fusion, f32[4,512,512]{1,2,0:T(8,128)S(1)} %fusion.76, f32[4,512]{1,0:T(4,128)S(1)} %multiply_bitcast_fusion, pred[512,512]{1,0:T(8,128)(4,1)S(1)} %iota_compare_fusion), kind=kOutput, calls=%fused_computation.35 | convolution fusion | flops 6444548096 | bytes 12853248 | tf_op jit(solution)/shard_map/vmap()/dot_general | solution.py:44
  243.3 5.1 fusion.51
  248.5 2.8 convolution_subtract_fusion.1
  252.6 3.6 fusion.94
  260.4 475.1 %while.26 = (s32[]{:T(128)}, bf16[2,4,512,128]{3,2,1,0:T(8,128)(2,1)}, bf16[4,128,128]{2,1,0:T(8,128)(2,1)}, f32[512]{0:T(512)S(1)}, f32[4,512,128]{2,1,0:T(8,12...) while((s32[]{:T(128)}, ...), condition=%wide.region_6.7_spmd, body=%wide.region_3.6_spmd.sunk | while | flops 952374272 | bytes 37763388 | solution.py:129
  260.6 3.6 collective-permute-start
  264.1 3.5 collective-permute-start.2
  267.7 3.2 collective-permute-start.1
  271.0 18.1 %collective-permute-done.2 = bf16[512]{0:T(512)(128)(2,1)S(1)} collective-permute-done((bf16[512]{0:T(512)(128)(2,1)S(1)}, bf16[512]{0:T(512)(128)(2,1)S(1)}, u32[]{:S(2)}, u32[]{:S(2)}) %collective-permute-start.2) | collective-permute-done | bytes 1056 | tf_op jit(solution)/shard_map/while/body/eval_jaxpr/ppermute | solution.py:14
  289.4 2.6 collective-permute-done.1
  300.7 2.7 collective-permute-start.2
  303.4 3.2 collective-permute-start.1
  306.8 19.5 %collective-permute-done.2 = bf16[512]{0:T(512)(128)(2,1)S(1)} collective-permute-done((bf16[512]{0:T(512)(128)(2,1)S(1)}, bf16[512]{0:T(512)(128)(2,1)S(1)}, u32[]{:S(2)}, u32[]{:S(2)}) %collective-permute-start.2) | collective-permute-done | bytes 1056 | tf_op jit(solution)/shard_map/while/body/eval_jaxpr/ppermute | solution.py:14
  326.5 2.6 collective-permute-done.1
  342.2 20.2 %collective-permute-done.2 = bf16[512]{0:T(512)(128)(2,1)S(1)} collective-permute-done((bf16[512]{0:T(512)(128)(2,1)S(1)}, bf16[512]{0:T(512)(128)(2,1)S(1)}, u32[]{:S(2)}, u32[]{:S(2)}) %collective-permute-start.2) | collective-permute-done | bytes 1056 | tf_op jit(solution)/shard_map/while/body/eval_jaxpr/ppermute | solution.py:14
  362.7 2.6 collective-permute-done.1
  375.9 2.5 collective-permute-start.1
  378.5 19.2 %collective-permute-done.2 = bf16[512]{0:T(512)(128)(2,1)S(1)} collective-permute-done((bf16[512]{0:T(512)(128)(2,1)S(1)}, bf16[512]{0:T(512)(128)(2,1)S(1)}, u32[]{:S(2)}, u32[]{:S(2)}) %collective-permute-start.2) | collective-permute-done | bytes 1056 | tf_op jit(solution)/shard_map/while/body/eval_jaxpr/ppermute | solution.py:14
  398.0 2.6 collective-permute-done.1
  411.2 2.6 collective-permute-start.1
  413.9 18.2 %collective-permute-done.2 = bf16[512]{0:T(512)(128)(2,1)S(1)} collective-permute-done((bf16[512]{0:T(512)(128)(2,1)S(1)}, bf16[512]{0:T(512)(128)(2,1)S(1)}, u32[]{:S(2)}, u32[]{:S(2)}) %collective-permute-start.2) | collective-permute-done | bytes 1056 | tf_op jit(solution)/shard_map/while/body/eval_jaxpr/ppermute | solution.py:14
  432.3 2.6 collective-permute-done.1
  445.5 2.7 collective-permute-start.1
  448.4 17.2 %collective-permute-done.2 = bf16[512]{0:T(512)(128)(2,1)S(1)} collective-permute-done((bf16[512]{0:T(512)(128)(2,1)S(1)}, bf16[512]{0:T(512)(128)(2,1)S(1)}, u32[]{:S(2)}, u32[]{:S(2)}) %collective-permute-start.2) | collective-permute-done | bytes 1056 | tf_op jit(solution)/shard_map/while/body/eval_jaxpr/ppermute | solution.py:14
  465.8 2.6 collective-permute-done.1
  479.0 2.8 collective-permute-start.1
  481.9 16.2 %collective-permute-done.2 = bf16[512]{0:T(512)(128)(2,1)S(1)} collective-permute-done((bf16[512]{0:T(512)(128)(2,1)S(1)}, bf16[512]{0:T(512)(128)(2,1)S(1)}, u32[]{:S(2)}, u32[]{:S(2)}) %collective-permute-start.2) | collective-permute-done | bytes 1056 | tf_op jit(solution)/shard_map/while/body/eval_jaxpr/ppermute | solution.py:14
  498.3 2.6 collective-permute-done.1
  511.5 2.9 collective-permute-start.1
  514.5 15.2 %collective-permute-done.2 = bf16[512]{0:T(512)(128)(2,1)S(1)} collective-permute-done((bf16[512]{0:T(512)(128)(2,1)S(1)}, bf16[512]{0:T(512)(128)(2,1)S(1)}, u32[]{:S(2)}, u32[]{:S(2)}) %collective-permute-start.2) | collective-permute-done | bytes 1056 | tf_op jit(solution)/shard_map/while/body/eval_jaxpr/ppermute | solution.py:14
  529.9 2.6 collective-permute-done.1
  543.1 2.9 collective-permute-start.1
  546.1 14.2 %collective-permute-done.2 = bf16[512]{0:T(512)(128)(2,1)S(1)} collective-permute-done((bf16[512]{0:T(512)(128)(2,1)S(1)}, bf16[512]{0:T(512)(128)(2,1)S(1)}, u32[]{:S(2)}, u32[]{:S(2)}) %collective-permute-start.2) | collective-permute-done | bytes 1056 | tf_op jit(solution)/shard_map/while/body/eval_jaxpr/ppermute | solution.py:14
  560.6 2.6 collective-permute-done.1
  573.8 3.0 collective-permute-start.1
  576.9 13.2 %collective-permute-done.2 = bf16[512]{0:T(512)(128)(2,1)S(1)} collective-permute-done((bf16[512]{0:T(512)(128)(2,1)S(1)}, bf16[512]{0:T(512)(128)(2,1)S(1)}, u32[]{:S(2)}, u32[]{:S(2)}) %collective-permute-start.2) | collective-permute-done | bytes 1056 | tf_op jit(solution)/shard_map/while/body/eval_jaxpr/ppermute | solution.py:14
  590.3 2.6 collective-permute-done.1
  603.5 3.1 collective-permute-start.1
  606.7 12.2 %collective-permute-done.2 = bf16[512]{0:T(512)(128)(2,1)S(1)} collective-permute-done((bf16[512]{0:T(512)(128)(2,1)S(1)}, bf16[512]{0:T(512)(128)(2,1)S(1)}, u32[]{:S(2)}, u32[]{:S(2)}) %collective-permute-start.2) | collective-permute-done | bytes 1056 | tf_op jit(solution)/shard_map/while/body/eval_jaxpr/ppermute | solution.py:14
  619.1 2.6 collective-permute-done.1
  632.4 3.2 collective-permute-start.1
  635.6 11.2 %collective-permute-done.2 = bf16[512]{0:T(512)(128)(2,1)S(1)} collective-permute-done((bf16[512]{0:T(512)(128)(2,1)S(1)}, bf16[512]{0:T(512)(128)(2,1)S(1)}, u32[]{:S(2)}, u32[]{:S(2)}) %collective-permute-start.2) | collective-permute-done | bytes 1056 | tf_op jit(solution)/shard_map/while/body/eval_jaxpr/ppermute | solution.py:14
  647.1 2.6 collective-permute-done.1
  660.3 3.2 collective-permute-start.1
  663.6 10.7 %collective-permute-done.2 = bf16[512]{0:T(512)(128)(2,1)S(1)} collective-permute-done((bf16[512]{0:T(512)(128)(2,1)S(1)}, bf16[512]{0:T(512)(128)(2,1)S(1)}, u32[]{:S(2)}, u32[]{:S(2)}) %collective-permute-start.2) | collective-permute-done | bytes 1056 | tf_op jit(solution)/shard_map/while/body/eval_jaxpr/ppermute | solution.py:14
  687.2 3.3 collective-permute-start.1
  690.7 10.6 %collective-permute-done.2 = bf16[512]{0:T(512)(128)(2,1)S(1)} collective-permute-done((bf16[512]{0:T(512)(128)(2,1)S(1)}, bf16[512]{0:T(512)(128)(2,1)S(1)}, u32[]{:S(2)}, u32[]{:S(2)}) %collective-permute-start.2) | collective-permute-done | bytes 1056 | tf_op jit(solution)/shard_map/while/body/eval_jaxpr/ppermute | solution.py:14
  713.3 3.6 collective-permute-start.1
  717.0 10.3 %collective-permute-done.2 = bf16[512]{0:T(512)(128)(2,1)S(1)} collective-permute-done((bf16[512]{0:T(512)(128)(2,1)S(1)}, bf16[512]{0:T(512)(128)(2,1)S(1)}, u32[]{:S(2)}, u32[]{:S(2)}) %collective-permute-start.2) | collective-permute-done | bytes 1056 | tf_op jit(solution)/shard_map/while/body/eval_jaxpr/ppermute | solution.py:14
  737.2 6.5 convolution_convert_fusion
  743.7 49.3 %reduce-scatter.2.cloned.1.call-done = bf16[64,4096]{1,0:T(8,128)(2,1)} async-done(((bf16[512,4096]{1,0:T(8,128)(2,1)}), bf16[64,4096]{1,0:T(8,128)(2,1)}) %reduce-scatter.2.cloned.1.call-update) | async-done | bytes 524304 | tf_op jit(solution)/shard_map/reduce_scatter | solution.py:133
  (362 shorter events, 193.8 us)
Async XLA Ops:
  6.5 786.5 %reduce-scatter.2.cloned.1.call-start = ((), (), s32[]{:S(2)}) async-start(), calls=%async_computation.1 | async-start | bytes 4718592 | tf_op jit(solution)/shard_map/reduce_scatter | solution.py:133
  7.8 5.9 copy-start.8
  13.6 205.3 %copy-start.1 = (bf16[512,4,128]{2,0,1:T(8,128)(2,1)}, bf16[512,4,128]{2,0,1:T(8,128)(2,1)S(1)}, u32[]{:S(2)}) copy-start(bf16[512,4,128]{2,0,1:T(8,128)(2,1)S(1)} %copy.23) | copy-start | bytes 1572868
  13.6 4.0 copy-start.4
  196.7 2.6 copy-start
  256.2 3.1 copy-start.7
  260.6 32.1 %collective-permute-start = (bf16[2,4,512,128]{3,2,1,0:T(8,128)(2,1)}, bf16[2,4,512,128]{3,2,1,0:T(8,128)(2,1)S(1)}, u32[]{:S(2)}, u32[]{:S(2)}) collective-permute-start(bf16[2,4,512,128]{3,2,1,0:T(8,128)(2,1)} %get-tuple-element.351), channel_id=1, source_target_pairs={{0,8},{8,16},{16,24},{24,32},{32,40},{40,48},{48,56},{56,64},{64,7... | collective-permute-start | bytes 3145736 | tf_op jit(solution)/shard_map/while/body/eval_jaxpr/ppermute | solution.py:14
  264.1 25.0 %collective-permute-start.2 = (bf16[512]{0:T(512)(128)(2,1)S(1)}, bf16[512]{0:T(512)(128)(2,1)S(1)}, u32[]{:S(2)}, u32[]{:S(2)}) collective-permute-start(bf16[512]{0:T(512)(128)(2,1)S(1)} %convert_element_type.126), channel_id=1, source_target_pairs={{0,8},{8,16},{16,24},{24,32},{32,40},{40,48},{48,56},{56,64},{64,7... | collective-permute-start | bytes 3080 | tf_op jit(solution)/shard_map/while/body/eval_jaxpr/ppermute | solution.py:14
  267.7 24.3 %collective-permute-start.1 = (bf16[4,128,128]{2,1,0:T(8,128)(2,1)}, bf16[4,128,128]{2,1,0:T(8,128)(2,1)S(1)}, u32[]{:S(2)}, u32[]{:S(2)}) collective-permute-start(bf16[4,128,128]{2,1,0:T(8,128)(2,1)} %get-tuple-element.352), channel_id=1, source_target_pairs={{0,8},{8,16},{16,24},{24,32},{32,40},{40,48},{48,56},{56,64},{64,7... | collective-permute-start | bytes 393224 | tf_op jit(solution)/shard_map/while/body/eval_jaxpr/ppermute | solution.py:14
  293.5 2.6 copy-start.5
  298.8 31.0 %collective-permute-start = (bf16[2,4,512,128]{3,2,1,0:T(8,128)(2,1)}, bf16[2,4,512,128]{3,2,1,0:T(8,128)(2,1)S(1)}, u32[]{:S(2)}, u32[]{:S(2)}) collective-permute-start(bf16[2,4,512,128]{3,2,1,0:T(8,128)(2,1)} %get-tuple-element.351), channel_id=1, source_target_pairs={{0,8},{8,16},{16,24},{24,32},{32,40},{40,48},{48,56},{56,64},{64,7... | collective-permute-start | bytes 3145736 | tf_op jit(solution)/shard_map/while/body/eval_jaxpr/ppermute | solution.py:14
  300.7 25.6 %collective-permute-start.2 = (bf16[512]{0:T(512)(128)(2,1)S(1)}, bf16[512]{0:T(512)(128)(2,1)S(1)}, u32[]{:S(2)}, u32[]{:S(2)}) collective-permute-start(bf16[512]{0:T(512)(128)(2,1)S(1)} %convert_element_type.126), channel_id=1, source_target_pairs={{0,8},{8,16},{16,24},{24,32},{32,40},{40,48},{48,56},{56,64},{64,7... | collective-permute-start | bytes 3080 | tf_op jit(solution)/shard_map/while/body/eval_jaxpr/ppermute | solution.py:14
  303.4 25.7 %collective-permute-start.1 = (bf16[4,128,128]{2,1,0:T(8,128)(2,1)}, bf16[4,128,128]{2,1,0:T(8,128)(2,1)S(1)}, u32[]{:S(2)}, u32[]{:S(2)}) collective-permute-start(bf16[4,128,128]{2,1,0:T(8,128)(2,1)} %get-tuple-element.352), channel_id=1, source_target_pairs={{0,8},{8,16},{16,24},{24,32},{32,40},{40,48},{48,56},{56,64},{64,7... | collective-permute-start | bytes 393224 | tf_op jit(solution)/shard_map/while/body/eval_jaxpr/ppermute | solution.py:14
  330.6 2.6 copy-start.5
  335.9 30.1 %collective-permute-start = (bf16[2,4,512,128]{3,2,1,0:T(8,128)(2,1)}, bf16[2,4,512,128]{3,2,1,0:T(8,128)(2,1)S(1)}, u32[]{:S(2)}, u32[]{:S(2)}) collective-permute-start(bf16[2,4,512,128]{3,2,1,0:T(8,128)(2,1)} %get-tuple-element.351), channel_id=1, source_target_pairs={{0,8},{8,16},{16,24},{24,32},{32,40},{40,48},{48,56},{56,64},{64,7... | collective-permute-start | bytes 3145736 | tf_op jit(solution)/shard_map/while/body/eval_jaxpr/ppermute | solution.py:14
  337.8 24.7 %collective-permute-start.2 = (bf16[512]{0:T(512)(128)(2,1)S(1)}, bf16[512]{0:T(512)(128)(2,1)S(1)}, u32[]{:S(2)}, u32[]{:S(2)}) collective-permute-start(bf16[512]{0:T(512)(128)(2,1)S(1)} %convert_element_type.126), channel_id=1, source_target_pairs={{0,8},{8,16},{16,24},{24,32},{32,40},{40,48},{48,56},{56,64},{64,7... | collective-permute-start | bytes 3080 | tf_op jit(solution)/shard_map/while/body/eval_jaxpr/ppermute | solution.py:14
  339.7 25.5 %collective-permute-start.1 = (bf16[4,128,128]{2,1,0:T(8,128)(2,1)}, bf16[4,128,128]{2,1,0:T(8,128)(2,1)S(1)}, u32[]{:S(2)}, u32[]{:S(2)}) collective-permute-start(bf16[4,128,128]{2,1,0:T(8,128)(2,1)} %get-tuple-element.352), channel_id=1, source_target_pairs={{0,8},{8,16},{16,24},{24,32},{32,40},{40,48},{48,56},{56,64},{64,7... | collective-permute-start | bytes 393224 | tf_op jit(solution)/shard_map/while/body/eval_jaxpr/ppermute | solution.py:14
  366.8 2.6 copy-start.5
  372.1 29.1 %collective-permute-start = (bf16[2,4,512,128]{3,2,1,0:T(8,128)(2,1)}, bf16[2,4,512,128]{3,2,1,0:T(8,128)(2,1)S(1)}, u32[]{:S(2)}, u32[]{:S(2)}) collective-permute-start(bf16[2,4,512,128]{3,2,1,0:T(8,128)(2,1)} %get-tuple-element.351), channel_id=1, source_target_pairs={{0,8},{8,16},{16,24},{24,32},{32,40},{40,48},{48,56},{56,64},{64,7... | collective-permute-start | bytes 3145736 | tf_op jit(solution)/shard_map/while/body/eval_jaxpr/ppermute | solution.py:14
  374.0 23.7 %collective-permute-start.2 = (bf16[512]{0:T(512)(128)(2,1)S(1)}, bf16[512]{0:T(512)(128)(2,1)S(1)}, u32[]{:S(2)}, u32[]{:S(2)}) collective-permute-start(bf16[512]{0:T(512)(128)(2,1)S(1)} %convert_element_type.126), channel_id=1, source_target_pairs={{0,8},{8,16},{16,24},{24,32},{32,40},{40,48},{48,56},{56,64},{64,7... | collective-permute-start | bytes 3080 | tf_op jit(solution)/shard_map/while/body/eval_jaxpr/ppermute | solution.py:14
  375.9 24.6 %collective-permute-start.1 = (bf16[4,128,128]{2,1,0:T(8,128)(2,1)}, bf16[4,128,128]{2,1,0:T(8,128)(2,1)S(1)}, u32[]{:S(2)}, u32[]{:S(2)}) collective-permute-start(bf16[4,128,128]{2,1,0:T(8,128)(2,1)} %get-tuple-element.352), channel_id=1, source_target_pairs={{0,8},{8,16},{16,24},{24,32},{32,40},{40,48},{48,56},{56,64},{64,7... | collective-permute-start | bytes 393224 | tf_op jit(solution)/shard_map/while/body/eval_jaxpr/ppermute | solution.py:14
  402.1 2.6 copy-start.5
  407.3 28.2 %collective-permute-start = (bf16[2,4,512,128]{3,2,1,0:T(8,128)(2,1)}, bf16[2,4,512,128]{3,2,1,0:T(8,128)(2,1)S(1)}, u32[]{:S(2)}, u32[]{:S(2)}) collective-permute-start(bf16[2,4,512,128]{3,2,1,0:T(8,128)(2,1)} %get-tuple-element.351), channel_id=1, source_target_pairs={{0,8},{8,16},{16,24},{24,32},{32,40},{40,48},{48,56},{56,64},{64,7... | collective-permute-start | bytes 3145736 | tf_op jit(solution)/shard_map/while/body/eval_jaxpr/ppermute | solution.py:14
  409.3 22.8 %collective-permute-start.2 = (bf16[512]{0:T(512)(128)(2,1)S(1)}, bf16[512]{0:T(512)(128)(2,1)S(1)}, u32[]{:S(2)}, u32[]{:S(2)}) collective-permute-start(bf16[512]{0:T(512)(128)(2,1)S(1)} %convert_element_type.126), channel_id=1, source_target_pairs={{0,8},{8,16},{16,24},{24,32},{32,40},{40,48},{48,56},{56,64},{64,7... | collective-permute-start | bytes 3080 | tf_op jit(solution)/shard_map/while/body/eval_jaxpr/ppermute | solution.py:14
  411.2 23.7 %collective-permute-start.1 = (bf16[4,128,128]{2,1,0:T(8,128)(2,1)}, bf16[4,128,128]{2,1,0:T(8,128)(2,1)S(1)}, u32[]{:S(2)}, u32[]{:S(2)}) collective-permute-start(bf16[4,128,128]{2,1,0:T(8,128)(2,1)} %get-tuple-element.352), channel_id=1, source_target_pairs={{0,8},{8,16},{16,24},{24,32},{32,40},{40,48},{48,56},{56,64},{64,7... | collective-permute-start | bytes 393224 | tf_op jit(solution)/shard_map/while/body/eval_jaxpr/ppermute | solution.py:14
  436.5 2.6 copy-start.5
  441.7 27.3 %collective-permute-start = (bf16[2,4,512,128]{3,2,1,0:T(8,128)(2,1)}, bf16[2,4,512,128]{3,2,1,0:T(8,128)(2,1)S(1)}, u32[]{:S(2)}, u32[]{:S(2)}) collective-permute-start(bf16[2,4,512,128]{3,2,1,0:T(8,128)(2,1)} %get-tuple-element.351), channel_id=1, source_target_pairs={{0,8},{8,16},{16,24},{24,32},{32,40},{40,48},{48,56},{56,64},{64,7... | collective-permute-start | bytes 3145736 | tf_op jit(solution)/shard_map/while/body/eval_jaxpr/ppermute | solution.py:14
  443.6 21.9 %collective-permute-start.2 = (bf16[512]{0:T(512)(128)(2,1)S(1)}, bf16[512]{0:T(512)(128)(2,1)S(1)}, u32[]{:S(2)}, u32[]{:S(2)}) collective-permute-start(bf16[512]{0:T(512)(128)(2,1)S(1)} %convert_element_type.126), channel_id=1, source_target_pairs={{0,8},{8,16},{16,24},{24,32},{32,40},{40,48},{48,56},{56,64},{64,7... | collective-permute-start | bytes 3080 | tf_op jit(solution)/shard_map/while/body/eval_jaxpr/ppermute | solution.py:14
  445.5 22.8 %collective-permute-start.1 = (bf16[4,128,128]{2,1,0:T(8,128)(2,1)}, bf16[4,128,128]{2,1,0:T(8,128)(2,1)S(1)}, u32[]{:S(2)}, u32[]{:S(2)}) collective-permute-start(bf16[4,128,128]{2,1,0:T(8,128)(2,1)} %get-tuple-element.352), channel_id=1, source_target_pairs={{0,8},{8,16},{16,24},{24,32},{32,40},{40,48},{48,56},{56,64},{64,7... | collective-permute-start | bytes 393224 | tf_op jit(solution)/shard_map/while/body/eval_jaxpr/ppermute | solution.py:14
  475.1 26.4 %collective-permute-start = (bf16[2,4,512,128]{3,2,1,0:T(8,128)(2,1)}, bf16[2,4,512,128]{3,2,1,0:T(8,128)(2,1)S(1)}, u32[]{:S(2)}, u32[]{:S(2)}) collective-permute-start(bf16[2,4,512,128]{3,2,1,0:T(8,128)(2,1)} %get-tuple-element.351), channel_id=1, source_target_pairs={{0,8},{8,16},{16,24},{24,32},{32,40},{40,48},{48,56},{56,64},{64,7... | collective-permute-start | bytes 3145736 | tf_op jit(solution)/shard_map/while/body/eval_jaxpr/ppermute | solution.py:14
  477.1 21.0 %collective-permute-start.2 = (bf16[512]{0:T(512)(128)(2,1)S(1)}, bf16[512]{0:T(512)(128)(2,1)S(1)}, u32[]{:S(2)}, u32[]{:S(2)}) collective-permute-start(bf16[512]{0:T(512)(128)(2,1)S(1)} %convert_element_type.126), channel_id=1, source_target_pairs={{0,8},{8,16},{16,24},{24,32},{32,40},{40,48},{48,56},{56,64},{64,7... | collective-permute-start | bytes 3080 | tf_op jit(solution)/shard_map/while/body/eval_jaxpr/ppermute | solution.py:14
  479.0 21.9 %collective-permute-start.1 = (bf16[4,128,128]{2,1,0:T(8,128)(2,1)}, bf16[4,128,128]{2,1,0:T(8,128)(2,1)S(1)}, u32[]{:S(2)}, u32[]{:S(2)}) collective-permute-start(bf16[4,128,128]{2,1,0:T(8,128)(2,1)} %get-tuple-element.352), channel_id=1, source_target_pairs={{0,8},{8,16},{16,24},{24,32},{32,40},{40,48},{48,56},{56,64},{64,7... | collective-permute-start | bytes 393224 | tf_op jit(solution)/shard_map/while/body/eval_jaxpr/ppermute | solution.py:14
  502.4 2.6 copy-start.5
  507.6 25.5 %collective-permute-start = (bf16[2,4,512,128]{3,2,1,0:T(8,128)(2,1)}, bf16[2,4,512,128]{3,2,1,0:T(8,128)(2,1)S(1)}, u32[]{:S(2)}, u32[]{:S(2)}) collective-permute-start(bf16[2,4,512,128]{3,2,1,0:T(8,128)(2,1)} %get-tuple-element.351), channel_id=1, source_target_pairs={{0,8},{8,16},{16,24},{24,32},{32,40},{40,48},{48,56},{56,64},{64,7... | collective-permute-start | bytes 3145736 | tf_op jit(solution)/shard_map/while/body/eval_jaxpr/ppermute | solution.py:14
  509.6 20.1 %collective-permute-start.2 = (bf16[512]{0:T(512)(128)(2,1)S(1)}, bf16[512]{0:T(512)(128)(2,1)S(1)}, u32[]{:S(2)}, u32[]{:S(2)}) collective-permute-start(bf16[512]{0:T(512)(128)(2,1)S(1)} %convert_element_type.126), channel_id=1, source_target_pairs={{0,8},{8,16},{16,24},{24,32},{32,40},{40,48},{48,56},{56,64},{64,7... | collective-permute-start | bytes 3080 | tf_op jit(solution)/shard_map/while/body/eval_jaxpr/ppermute | solution.py:14
  511.5 20.9 %collective-permute-start.1 = (bf16[4,128,128]{2,1,0:T(8,128)(2,1)}, bf16[4,128,128]{2,1,0:T(8,128)(2,1)S(1)}, u32[]{:S(2)}, u32[]{:S(2)}) collective-permute-start(bf16[4,128,128]{2,1,0:T(8,128)(2,1)} %get-tuple-element.352), channel_id=1, source_target_pairs={{0,8},{8,16},{16,24},{24,32},{32,40},{40,48},{48,56},{56,64},{64,7... | collective-permute-start | bytes 393224 | tf_op jit(solution)/shard_map/while/body/eval_jaxpr/ppermute | solution.py:14
  534.0 2.6 copy-start.5
  539.2 24.5 %collective-permute-start = (bf16[2,4,512,128]{3,2,1,0:T(8,128)(2,1)}, bf16[2,4,512,128]{3,2,1,0:T(8,128)(2,1)S(1)}, u32[]{:S(2)}, u32[]{:S(2)}) collective-permute-start(bf16[2,4,512,128]{3,2,1,0:T(8,128)(2,1)} %get-tuple-element.351), channel_id=1, source_target_pairs={{0,8},{8,16},{16,24},{24,32},{32,40},{40,48},{48,56},{56,64},{64,7... | collective-permute-start | bytes 3145736 | tf_op jit(solution)/shard_map/while/body/eval_jaxpr/ppermute | solution.py:14
  541.2 19.1 %collective-permute-start.2 = (bf16[512]{0:T(512)(128)(2,1)S(1)}, bf16[512]{0:T(512)(128)(2,1)S(1)}, u32[]{:S(2)}, u32[]{:S(2)}) collective-permute-start(bf16[512]{0:T(512)(128)(2,1)S(1)} %convert_element_type.126), channel_id=1, source_target_pairs={{0,8},{8,16},{16,24},{24,32},{32,40},{40,48},{48,56},{56,64},{64,7... | collective-permute-start | bytes 3080 | tf_op jit(solution)/shard_map/while/body/eval_jaxpr/ppermute | solution.py:14
  543.1 20.0 %collective-permute-start.1 = (bf16[4,128,128]{2,1,0:T(8,128)(2,1)}, bf16[4,128,128]{2,1,0:T(8,128)(2,1)S(1)}, u32[]{:S(2)}, u32[]{:S(2)}) collective-permute-start(bf16[4,128,128]{2,1,0:T(8,128)(2,1)} %get-tuple-element.352), channel_id=1, source_target_pairs={{0,8},{8,16},{16,24},{24,32},{32,40},{40,48},{48,56},{56,64},{64,7... | collective-permute-start | bytes 393224 | tf_op jit(solution)/shard_map/while/body/eval_jaxpr/ppermute | solution.py:14
  564.7 2.6 copy-start.5
  569.9 23.6 %collective-permute-start = (bf16[2,4,512,128]{3,2,1,0:T(8,128)(2,1)}, bf16[2,4,512,128]{3,2,1,0:T(8,128)(2,1)S(1)}, u32[]{:S(2)}, u32[]{:S(2)}) collective-permute-start(bf16[2,4,512,128]{3,2,1,0:T(8,128)(2,1)} %get-tuple-element.351), channel_id=1, source_target_pairs={{0,8},{8,16},{16,24},{24,32},{32,40},{40,48},{48,56},{56,64},{64,7... | collective-permute-start | bytes 3145736 | tf_op jit(solution)/shard_map/while/body/eval_jaxpr/ppermute | solution.py:14
  571.8 18.2 %collective-permute-start.2 = (bf16[512]{0:T(512)(128)(2,1)S(1)}, bf16[512]{0:T(512)(128)(2,1)S(1)}, u32[]{:S(2)}, u32[]{:S(2)}) collective-permute-start(bf16[512]{0:T(512)(128)(2,1)S(1)} %convert_element_type.126), channel_id=1, source_target_pairs={{0,8},{8,16},{16,24},{24,32},{32,40},{40,48},{48,56},{56,64},{64,7... | collective-permute-start | bytes 3080 | tf_op jit(solution)/shard_map/while/body/eval_jaxpr/ppermute | solution.py:14
  573.8 19.1 %collective-permute-start.1 = (bf16[4,128,128]{2,1,0:T(8,128)(2,1)}, bf16[4,128,128]{2,1,0:T(8,128)(2,1)S(1)}, u32[]{:S(2)}, u32[]{:S(2)}) collective-permute-start(bf16[4,128,128]{2,1,0:T(8,128)(2,1)} %get-tuple-element.352), channel_id=1, source_target_pairs={{0,8},{8,16},{16,24},{24,32},{32,40},{40,48},{48,56},{56,64},{64,7... | collective-permute-start | bytes 393224 | tf_op jit(solution)/shard_map/while/body/eval_jaxpr/ppermute | solution.py:14
  594.4 2.6 copy-start.5
  599.7 22.7 %collective-permute-start = (bf16[2,4,512,128]{3,2,1,0:T(8,128)(2,1)}, bf16[2,4,512,128]{3,2,1,0:T(8,128)(2,1)S(1)}, u32[]{:S(2)}, u32[]{:S(2)}) collective-permute-start(bf16[2,4,512,128]{3,2,1,0:T(8,128)(2,1)} %get-tuple-element.351), channel_id=1, source_target_pairs={{0,8},{8,16},{16,24},{24,32},{32,40},{40,48},{48,56},{56,64},{64,7... | collective-permute-start | bytes 3145736 | tf_op jit(solution)/shard_map/while/body/eval_jaxpr/ppermute | solution.py:14
  601.6 17.3 %collective-permute-start.2 = (bf16[512]{0:T(512)(128)(2,1)S(1)}, bf16[512]{0:T(512)(128)(2,1)S(1)}, u32[]{:S(2)}, u32[]{:S(2)}) collective-permute-start(bf16[512]{0:T(512)(128)(2,1)S(1)} %convert_element_type.126), channel_id=1, source_target_pairs={{0,8},{8,16},{16,24},{24,32},{32,40},{40,48},{48,56},{56,64},{64,7... | collective-permute-start | bytes 3080 | tf_op jit(solution)/shard_map/while/body/eval_jaxpr/ppermute | solution.py:14
  603.5 18.2 %collective-permute-start.1 = (bf16[4,128,128]{2,1,0:T(8,128)(2,1)}, bf16[4,128,128]{2,1,0:T(8,128)(2,1)S(1)}, u32[]{:S(2)}, u32[]{:S(2)}) collective-permute-start(bf16[4,128,128]{2,1,0:T(8,128)(2,1)} %get-tuple-element.352), channel_id=1, source_target_pairs={{0,8},{8,16},{16,24},{24,32},{32,40},{40,48},{48,56},{56,64},{64,7... | collective-permute-start | bytes 393224 | tf_op jit(solution)/shard_map/while/body/eval_jaxpr/ppermute | solution.py:14
  623.3 2.6 copy-start.5
  628.5 21.8 %collective-permute-start = (bf16[2,4,512,128]{3,2,1,0:T(8,128)(2,1)}, bf16[2,4,512,128]{3,2,1,0:T(8,128)(2,1)S(1)}, u32[]{:S(2)}, u32[]{:S(2)}) collective-permute-start(bf16[2,4,512,128]{3,2,1,0:T(8,128)(2,1)} %get-tuple-element.351), channel_id=1, source_target_pairs={{0,8},{8,16},{16,24},{24,32},{32,40},{40,48},{48,56},{56,64},{64,7... | collective-permute-start | bytes 3145736 | tf_op jit(solution)/shard_map/while/body/eval_jaxpr/ppermute | solution.py:14
  630.4 16.4 %collective-permute-start.2 = (bf16[512]{0:T(512)(128)(2,1)S(1)}, bf16[512]{0:T(512)(128)(2,1)S(1)}, u32[]{:S(2)}, u32[]{:S(2)}) collective-permute-start(bf16[512]{0:T(512)(128)(2,1)S(1)} %convert_element_type.126), channel_id=1, source_target_pairs={{0,8},{8,16},{16,24},{24,32},{32,40},{40,48},{48,56},{56,64},{64,7... | collective-permute-start | bytes 3080 | tf_op jit(solution)/shard_map/while/body/eval_jaxpr/ppermute | solution.py:14
  632.4 17.3 %collective-permute-start.1 = (bf16[4,128,128]{2,1,0:T(8,128)(2,1)}, bf16[4,128,128]{2,1,0:T(8,128)(2,1)S(1)}, u32[]{:S(2)}, u32[]{:S(2)}) collective-permute-start(bf16[4,128,128]{2,1,0:T(8,128)(2,1)} %get-tuple-element.352), channel_id=1, source_target_pairs={{0,8},{8,16},{16,24},{24,32},{32,40},{40,48},{48,56},{56,64},{64,7... | collective-permute-start | bytes 393224 | tf_op jit(solution)/shard_map/while/body/eval_jaxpr/ppermute | solution.py:14
  651.2 2.6 copy-start.5
  656.4 20.8 %collective-permute-start = (bf16[2,4,512,128]{3,2,1,0:T(8,128)(2,1)}, bf16[2,4,512,128]{3,2,1,0:T(8,128)(2,1)S(1)}, u32[]{:S(2)}, u32[]{:S(2)}) collective-permute-start(bf16[2,4,512,128]{3,2,1,0:T(8,128)(2,1)} %get-tuple-element.351), channel_id=1, source_target_pairs={{0,8},{8,16},{16,24},{24,32},{32,40},{40,48},{48,56},{56,64},{64,7... | collective-permute-start | bytes 3145736 | tf_op jit(solution)/shard_map/while/body/eval_jaxpr/ppermute | solution.py:14
  658.3 16.0 %collective-permute-start.2 = (bf16[512]{0:T(512)(128)(2,1)S(1)}, bf16[512]{0:T(512)(128)(2,1)S(1)}, u32[]{:S(2)}, u32[]{:S(2)}) collective-permute-start(bf16[512]{0:T(512)(128)(2,1)S(1)} %convert_element_type.126), channel_id=1, source_target_pairs={{0,8},{8,16},{16,24},{24,32},{32,40},{40,48},{48,56},{56,64},{64,7... | collective-permute-start | bytes 3080 | tf_op jit(solution)/shard_map/while/body/eval_jaxpr/ppermute | solution.py:14
  660.3 16.3 %collective-permute-start.1 = (bf16[4,128,128]{2,1,0:T(8,128)(2,1)}, bf16[4,128,128]{2,1,0:T(8,128)(2,1)S(1)}, u32[]{:S(2)}, u32[]{:S(2)}) collective-permute-start(bf16[4,128,128]{2,1,0:T(8,128)(2,1)} %get-tuple-element.352), channel_id=1, source_target_pairs={{0,8},{8,16},{16,24},{24,32},{32,40},{40,48},{48,56},{56,64},{64,7... | collective-permute-start | bytes 393224 | tf_op jit(solution)/shard_map/while/body/eval_jaxpr/ppermute | solution.py:14
  678.1 2.6 copy-start.5
  683.4 19.9 %collective-permute-start = (bf16[2,4,512,128]{3,2,1,0:T(8,128)(2,1)}, bf16[2,4,512,128]{3,2,1,0:T(8,128)(2,1)S(1)}, u32[]{:S(2)}, u32[]{:S(2)}) collective-permute-start(bf16[2,4,512,128]{3,2,1,0:T(8,128)(2,1)} %get-tuple-element.351), channel_id=1, source_target_pairs={{0,8},{8,16},{16,24},{24,32},{32,40},{40,48},{48,56},{56,64},{64,7... | collective-permute-start | bytes 3145736 | tf_op jit(solution)/shard_map/while/body/eval_jaxpr/ppermute | solution.py:14
  685.3 16.0 %collective-permute-start.2 = (bf16[512]{0:T(512)(128)(2,1)S(1)}, bf16[512]{0:T(512)(128)(2,1)S(1)}, u32[]{:S(2)}, u32[]{:S(2)}) collective-permute-start(bf16[512]{0:T(512)(128)(2,1)S(1)} %convert_element_type.126), channel_id=1, source_target_pairs={{0,8},{8,16},{16,24},{24,32},{32,40},{40,48},{48,56},{56,64},{64,7... | collective-permute-start | bytes 3080 | tf_op jit(solution)/shard_map/while/body/eval_jaxpr/ppermute | solution.py:14
  687.2 15.4 %collective-permute-start.1 = (bf16[4,128,128]{2,1,0:T(8,128)(2,1)}, bf16[4,128,128]{2,1,0:T(8,128)(2,1)S(1)}, u32[]{:S(2)}, u32[]{:S(2)}) collective-permute-start(bf16[4,128,128]{2,1,0:T(8,128)(2,1)} %get-tuple-element.352), channel_id=1, source_target_pairs={{0,8},{8,16},{16,24},{24,32},{32,40},{40,48},{48,56},{56,64},{64,7... | collective-permute-start | bytes 393224 | tf_op jit(solution)/shard_map/while/body/eval_jaxpr/ppermute | solution.py:14
  704.2 2.6 copy-start.5
  709.4 19.9 %collective-permute-start = (bf16[2,4,512,128]{3,2,1,0:T(8,128)(2,1)}, bf16[2,4,512,128]{3,2,1,0:T(8,128)(2,1)S(1)}, u32[]{:S(2)}, u32[]{:S(2)}) collective-permute-start(bf16[2,4,512,128]{3,2,1,0:T(8,128)(2,1)} %get-tuple-element.351), channel_id=1, source_target_pairs={{0,8},{8,16},{16,24},{24,32},{32,40},{40,48},{48,56},{56,64},{64,7... | collective-permute-start | bytes 3145736 | tf_op jit(solution)/shard_map/while/body/eval_jaxpr/ppermute | solution.py:14
  711.4 16.0 %collective-permute-start.2 = (bf16[512]{0:T(512)(128)(2,1)S(1)}, bf16[512]{0:T(512)(128)(2,1)S(1)}, u32[]{:S(2)}, u32[]{:S(2)}) collective-permute-start(bf16[512]{0:T(512)(128)(2,1)S(1)} %convert_element_type.126), channel_id=1, source_target_pairs={{0,8},{8,16},{16,24},{24,32},{32,40},{40,48},{48,56},{56,64},{64,7... | collective-permute-start | bytes 3080 | tf_op jit(solution)/shard_map/while/body/eval_jaxpr/ppermute | solution.py:14
  713.3 15.4 %collective-permute-start.1 = (bf16[4,128,128]{2,1,0:T(8,128)(2,1)}, bf16[4,128,128]{2,1,0:T(8,128)(2,1)S(1)}, u32[]{:S(2)}, u32[]{:S(2)}) collective-permute-start(bf16[4,128,128]{2,1,0:T(8,128)(2,1)} %get-tuple-element.352), channel_id=1, source_target_pairs={{0,8},{8,16},{16,24},{24,32},{32,40},{40,48},{48,56},{56,64},{64,7... | collective-permute-start | bytes 393224 | tf_op jit(solution)/shard_map/while/body/eval_jaxpr/ppermute | solution.py:14
  (20 other events, 23.4 us)
Sparse Core Ops, SparseCore 0:
  743.8 49.1 reduce-scatter.1
where the time goes:
time: 812 us; the launch traced here: 800 us
  waiting for transfers between devices  311 us (38%)
  other arithmetic  184 us (23%)
  matrix products  115 us (14%)
  starting transfers between devices  106 us (13%)
  local copies, waits for them, and re-layouts  68.2 us (8%)
  between operations  13.9 us (2%)
    ppermute x45, waiting for transfers between devices, shifted(): lax.ppermute(value, axis, [(source, source + steps) for source in range(f...  261 us
    another operation x4, other arithmetic, shard_operators(): lax.linalg.triangular_solve(unit_lower, jnp.concatenate([key_proj, vector...  161 us
    ppermute x45, starting transfers between devices, shifted(): lax.ppermute(value, axis, [(source, source + steps) for source in range(f...  106 us
    reduce_scatter x1, waiting for transfers between devices, on_device(): lax.psum_scatter(jnp.dot(token_rows, out_weight, preferred_element_type=j...  49.3 us
    while x120, local copies, waits for them, and re-layouts  40.9 us
    dot_general x15, matrix products, attend(): jnp.einsum('hqk,hkd->hqd', weights.astype(jnp.bfloat16), key_pair[1], pre...  24.7 us
  transfers between devices with their start and end apart: 46, of which 31 were waited for; matrix products, arithmetic and copies ran while one was open for 2% of the time, Pallas kernels for 0%

commit v1 on v0

v1 whole, which is shorter than its diff:
```python
import functools
import math

import jax
import jax.numpy as jnp
from jax import lax
from jax.experimental import pallas as pl
from jax.experimental.pallas import tpu as pltpu
from jax.sharding import PartitionSpec as P

MESH = pl.DeviceIdType.MESH
F32 = jnp.float32
BF16 = jnp.bfloat16

HEAD = 128
BLOCK = 512
SUB = 128
N_SUB = 4
N_HEAD = 4
GROUP = 4
TILE = 256
NEG = -1e30
UNIT = math.log2(math.e) / math.sqrt(HEAD)

AT_Q, AT_K, AT_V, AT_T, AT_D = 0, 512, 1024, 1536, 1664
PACKET = 1680
PART = BLOCK + 16
PART_HALF = TILE + 16


def nn(a, b):
    return lax.dot_general(a, b, (((1,), (0,)), ((), ())), preferred_element_type=F32)


def nt(a, b):
    return lax.dot_general(a, b, (((1,), (1,)), ((), ())), preferred_element_type=F32)


def halves(a):
    high = a.astype(BF16)
    return high, (a - high.astype(F32)).astype(BF16)


def rows_to_column(row, eye):
    return jnp.sum(jnp.where(eye, row, 0.0), axis=1, keepdims=True)


def column_to_rows(column, eye):
    return jnp.sum(jnp.where(eye, column, 0.0), axis=0, keepdims=True)


def pieces(rows):
    high = rows.astype(BF16).astype(F32)
    rest = rows - high
    middle = rest.astype(BF16).astype(F32)
    low = rest - middle
    pad = jnp.zeros((16 - 3 * rows.shape[0], rows.shape[1]), F32)
    return jnp.concatenate([high, middle, low, pad], axis=0).astype(BF16)


def unpieced(tail, count):
    tail = tail.astype(F32)
    return tail[:count] + tail[count : 2 * count] + tail[2 * count : 3 * count]


def identity_masks():
    row = lax.broadcasted_iota(jnp.int32, (SUB, SUB), 0)
    col = lax.broadcasted_iota(jnp.int32, (SUB, SUB), 1)
    return row, col


def attention_kernel(
    q_ref, k_ref, v_ref, u_ref, logit_ref, doc_ref, out_ref,
    level_ref, beta_ref, packet_out, packet_in, turned_ref, forward_ref, cross_in, lone_in, lone_out,
    part_in_out, part_cross_out, part_lone_out, part_in, part_cross, part_lone, log_ref,
    acc_ref, max_ref, sum_ref,
    own_sem, pk_send, pk_recv, xf_send, xf_recv, lone_send, lone_recv,
    pi_send, pi_recv, pc_send, pc_recv, pl_send, pl_recv,
):
    me = lax.axis_index("ctx")
    n_ctx = lax.axis_size("ctx")
    x = me // GROUP
    z = lax.rem(me, GROUP)
    base = x * GROUP

    barrier = pltpu.get_barrier_semaphore()

    def greet(step, carry):
        pl.semaphore_signal(barrier, inc=1, device_id={"ctx": lax.rem(me + step, n_ctx)}, device_id_type=MESH)
        return carry

    lax.fori_loop(1, n_ctx, greet, 0)

    row, col = identity_masks()
    for level in range(7):
        hit = ((row >> level) + 1 == (col >> level)) & (((row >> level) & 1) == 0)
        level_ref[level] = jnp.where(hit, 1.0, 0.0).astype(BF16)
    beta_ref[...] = 2.0 * jax.nn.sigmoid(logit_ref[...])

    def send_packet(head):
        return pltpu.make_async_remote_copy(
            src_ref=packet_out.at[head], dst_ref=packet_in.at[z],
            send_sem=pk_send.at[head], recv_sem=pk_recv.at[z],
            device_id={"ctx": base + head}, device_id_type=MESH,
        )

    def head_step(turn, carry):
        head = lax.rem(z + 1 + turn, N_HEAD)
        lanes = pl.ds(pl.multiple_of(head * HEAD, HEAD), HEAD)
        row, col = identity_masks()
        eye = row == col
        upper = col > row
        lower = col < row
        causal = col <= row
        one = jnp.where(eye, 1.0, 0.0)
        lane4 = lax.broadcasted_iota(jnp.int32, (BLOCK, N_HEAD), 1)
        beta = jnp.sum(jnp.where(lane4 == head, beta_ref[...], 0.0), axis=1, keepdims=True)
        subs = range(N_SUB)
        at = [slice(a * SUB, (a + 1) * SUB) for a in subs]
        q = [q_ref[at[a], lanes] for a in subs]
        k = [k_ref[at[a], lanes] for a in subs]
        v = [v_ref[at[a], lanes] for a in subs]
        u = [u_ref[at[a], lanes] for a in subs]
        tau, tau_row, lt, low_t, lt_low, skew_t, qk, skew, aq = [], [], [], [], [], [], [], [], []
        for a in subs:
            wide = u[a].astype(F32)
            tau.append(beta[at[a]] / (jnp.sum(wide * wide, axis=1, keepdims=True) + 1e-6))
            tau_row.append(column_to_rows(tau[a], eye))
            gram = jnp.where(upper, nt(u[a], u[a]) * tau[a], 0.0)
            high, low = halves(gram)
            lt.append(high)
            lt_low.append(low)
        inverse = []
        for a in subs:
            inverse.append((one - (lt[a] * level_ref[0]).astype(F32)).astype(BF16))
        for level in range(1, 7):
            first = [nn(inverse[a], lt[a] * level_ref[level]).astype(BF16) for a in subs]
            inverse = [
                (inverse[a].astype(F32) - nn(first[a], inverse[a])).astype(BF16) for a in subs
            ]
        residual = [
            (one - inverse[a].astype(F32) - (nn(lt[a], inverse[a]) + nn(lt_low[a], inverse[a]))).astype(BF16)
            for a in subs
        ]
        solved = [inverse[a].astype(F32) + nn(inverse[a], residual[a]) for a in subs]
        z_full, trans, keys, intra, turned = [], [], [], [], []
        for a in subs:
            high, low = halves(solved[a] * tau_row[a])
            z_full.append(nn(high, u[a]) + nn(low, u[a]))
        for a in subs:
            high, low = halves(z_full[a])
            across = u[a].astype(F32).T.astype(BF16)
            trans.append(one - (nn(across, high) + nn(across, low)))
            skew_t = jnp.where(upper, nt(k[a], u[a]), 0.0).astype(BF16)
            keys.append(k[a].astype(F32) - nn(skew_t, high))
        for a in subs:
            a_high, a_low = halves(jnp.where(causal, nt(q[a], u[a]), 0.0) * tau_row[a])
            s_high, s_low = halves(solved[a])
            y = (nt(a_high, s_high) + nt(a_low, s_high) + nt(a_high, s_low)).astype(BF16)
            skew = jnp.where(lower, nt(u[a], k[a]), 0.0).astype(BF16)
            intra.append((nt(q[a], k[a]) - nn(y, skew)) * UNIT)
            turned.append((q[a].astype(F32) - nn(y, u[a])) * UNIT)

        def as_b(value):
            return value.astype(BF16)

        t_b = [as_b(trans[a]) for a in subs]
        near_10 = nt(as_b(turned[1]), as_b(keys[0]))
        near_32 = nt(as_b(turned[3]), as_b(keys[2]))
        turned[1] = nt(as_b(turned[1]), t_b[0])
        turned[3] = nt(as_b(turned[3]), t_b[2])
        keys[0] = nn(as_b(keys[0]), t_b[1])
        keys[2] = nn(as_b(keys[2]), t_b[3])

        def product(left, right):
            left_high, left_low = halves(left)
            right_high, right_low = halves(right)
            return nn(left_high, right_high) + nn(left_low, right_high) + nn(left_high, right_low)

        pair_a = product(trans[0], trans[1])
        pair_b = product(trans[2], trans[3])
        late = jnp.concatenate([as_b(turned[2]), as_b(turned[3])], axis=0)
        early = jnp.concatenate([as_b(keys[0]), as_b(keys[1])], axis=0)
        far = nt(late, early)
        late = nt(late, as_b(pair_a))
        early = nn(early, as_b(pair_b))
        whole = product(pair_a, pair_b)
        packet_out[head, AT_Q : AT_Q + 256] = as_b(jnp.concatenate([turned[0], turned[1]], axis=0))
        packet_out[head, AT_Q + 256 : AT_Q + 512] = as_b(late)
        packet_out[head, AT_K : AT_K + 256] = as_b(early)
        packet_out[head, AT_K + 256 : AT_K + 512] = as_b(jnp.concatenate([keys[2], keys[3]], axis=0))
        packet_out[head, AT_V : AT_V + 512] = jnp.concatenate(v, axis=0)
        packet_out[head, AT_T : AT_T + 128] = as_b(whole)
        docs = doc_ref[...]
        packet_out[head, AT_D : AT_D + 16] = as_b(
            jnp.concatenate([docs, jnp.zeros((16 - N_SUB, SUB), F32)], axis=0)
        )

        @pl.when(turn == 0)
        def _():
            pl.semaphore_wait(barrier, n_ctx - 1)

        @pl.when(turn < N_HEAD - 1)
        def _():
            send_packet(head).start()

        tiles = [
            [intra[0]],
            [near_10, intra[1]],
            [far[:SUB, :SUB], far[:SUB, SUB:], intra[2]],
            [far[SUB:, :SUB], far[SUB:, SUB:], near_32, intra[3]],
        ]
        for a in subs:
            mine = rows_to_column(docs[a : a + 1], eye)
            scores = []
            for b in range(a + 1):
                allowed = mine == docs[b : b + 1]
                if b == a:
                    allowed = allowed & causal
                scores.append(jnp.where(allowed, tiles[a][b], NEG))
            top = scores[0]
            for score in scores[1:]:
                top = jnp.maximum(top, score)
            top = jnp.max(top, axis=1, keepdims=True)
            weights = [jnp.exp2(score - top) for score in scores]
            total = weights[0]
            for weight in weights[1:]:
                total = total + weight
            total = jnp.sum(total, axis=1, keepdims=True)
            joined = jnp.concatenate([as_b(weight) for weight in weights], axis=1)
            acc_ref[head, at[a]] = nn(joined, jnp.concatenate(v[: a + 1], axis=0))
            max_ref[head, at[a]] = jnp.broadcast_to(top, (SUB, HEAD))
            sum_ref[head, at[a]] = jnp.broadcast_to(total, (SUB, HEAD))
        return carry

    lax.fori_loop(0, N_HEAD, head_step, 0)

    own = pltpu.make_async_copy(packet_out.at[z], packet_in.at[z], own_sem)
    own.start()
    own.wait()

    def packet_arrival(slot):
        return pltpu.make_async_remote_copy(
            src_ref=packet_out.at[slot], dst_ref=packet_in.at[slot],
            send_sem=pk_send.at[slot], recv_sem=pk_recv.at[slot],
            device_id={"ctx": base + slot}, device_id_type=MESH,
        )

    for slot in range(GROUP):
        @pl.when(slot != z)
        def _():
            packet_arrival(slot).wait_recv()

    def transition(slot):
        return packet_in[slot, AT_T : AT_T + 128]

    def send_forward(slot):
        return pltpu.make_async_remote_copy(
            src_ref=forward_ref.at[slot], dst_ref=cross_in.at[slot],
            send_sem=xf_send.at[slot], recv_sem=xf_recv.at[slot],
            device_id={"ctx": lax.rem(me + n_ctx - GROUP, n_ctx)}, device_id_type=MESH,
        )

    def send_lone():
        return pltpu.make_async_remote_copy(
            src_ref=lone_out, dst_ref=lone_in,
            send_sem=lone_send, recv_sem=lone_recv,
            device_id={"ctx": lax.rem(me + n_ctx - GROUP, n_ctx)}, device_id_type=MESH,
        )

    @pl.when(x == 2)
    def _():
        lone_out[...] = packet_in[0, AT_Q : AT_Q + TILE]
        send_lone().start()

    is_odd = lax.rem(x, 2) == 1
    for slot in range(GROUP):
        value = packet_in[slot, AT_Q : AT_Q + BLOCK]
        for source in range(slot - 1, -1, -1):
            turned_ref[slot * (slot - 1) // 2 + source] = value
            if source > 0:
                value = nt(value, transition(source)).astype(BF16)

        @pl.when(is_odd)
        def _():
            last = value if slot == 0 else nt(value, transition(0)).astype(BF16)
            forward_ref[slot, 0:BLOCK] = last
            forward_ref[slot, BLOCK:] = packet_in[slot, AT_D : AT_D + 16]
            send_forward(slot).start()

    row, col = identity_masks()
    eye = row == col

    def key_documents(slot):
        docs = packet_in[slot, AT_D : AT_D + 16].astype(F32)
        return [docs[a : a + 1] for a in range(N_SUB)]

    def attend(turned, slots, query_docs):
        scores = []
        for value, slot in zip(turned, slots):
            raw = nt(value, packet_in[slot, AT_K : AT_K + BLOCK])
            for a, docs in enumerate(key_documents(slot)):
                scores.append(jnp.where(query_docs == docs, raw[:, a * SUB : (a + 1) * SUB], NEG))
        top = scores[0]
        for score in scores[1:]:
            top = jnp.maximum(top, score)
        top = jnp.max(top, axis=1, keepdims=True)
        total = None
        mixed = None
        for index, slot in enumerate(slots):
            weights = [jnp.exp2(score - top) for score in scores[index * N_SUB : (index + 1) * N_SUB]]
            for weight in weights:
                total = weight if total is None else total + weight
            joined = jnp.concatenate([weight.astype(BF16) for weight in weights], axis=1)
            term = nn(joined, packet_in[slot, AT_V : AT_V + BLOCK])
            mixed = term if mixed is None else mixed + term
        total = jnp.sum(total, axis=1, keepdims=True)
        return (mixed / total).astype(BF16), top + jnp.log2(total)

    def query_documents(docs, tile):
        columns = [rows_to_column(docs[a : a + 1], eye) for a in range(2)]
        return jnp.concatenate(columns, axis=0)

    def log_rows(log_sum):
        return jnp.concatenate(
            [column_to_rows(log_sum[a * SUB : (a + 1) * SUB], eye) for a in range(2)], axis=0
        )

    def send_part_in(slot):
        return pltpu.make_async_remote_copy(
            src_ref=part_in_out.at[slot], dst_ref=part_in.at[z],
            send_sem=pi_send.at[slot], recv_sem=pi_recv.at[z],
            device_id={"ctx": base + slot}, device_id_type=MESH,
        )

    for slot in range(1, GROUP):
        docs = packet_in[slot, AT_D : AT_D + 16].astype(F32)
        logs = []
        for tile in range(BLOCK // TILE):
            at = slice(tile * TILE, (tile + 1) * TILE)
            sources = list(range(slot - 1, -1, -1))
            turned = [turned_ref[slot * (slot - 1) // 2 + source, at] for source in sources]
            mixed, log_sum = attend(turned, sources, query_documents(docs[2 * tile : 2 * tile + 2], tile))
            part_in_out[slot, at] = mixed
            logs.append(log_rows(log_sum))
        part_in_out[slot, BLOCK:] = pieces(jnp.concatenate(logs, axis=0))

        @pl.when(slot != z)
        def _():
            send_part_in(slot).start()

        @pl.when(slot == z)
        def _():
            part_in[z] = part_in_out[slot]

    every = list(range(GROUP - 1, -1, -1))

    def chain(value):
        turned = [value]
        for source in every[:-1]:
            turned.append(nt(turned[-1], transition(source)).astype(BF16))
        return turned

    def send_part_lone(which):
        return pltpu.make_async_remote_copy(
            src_ref=part_lone_out, dst_ref=part_lone.at[which, z],
            send_sem=pl_send, recv_sem=pl_recv.at[which, z],
            device_id={"ctx": 2 * GROUP}, device_id_type=MESH,
        )

    def lone_rows(hand_down):
        send_lone().wait_recv()
        turned = chain(lone_in[...])
        if hand_down:
            lone_out[...] = nt(turned[-1], transition(0)).astype(BF16)
            send_lone().start()
        mixed, log_sum = attend(turned, every, jnp.zeros((TILE, 1), F32))
        part_lone_out[0:TILE] = mixed
        part_lone_out[TILE:] = pieces(log_rows(log_sum))

    @pl.when(x == 1)
    def _():
        lone_rows(True)
        send_part_lone(0).start()

    def send_part_cross(slot):
        return pltpu.make_async_remote_copy(
            src_ref=part_cross_out.at[slot], dst_ref=part_cross.at[z],
            send_sem=pc_send.at[slot], recv_sem=pc_recv.at[z],
            device_id={"ctx": base + GROUP + slot}, device_id_type=MESH,
        )

    @pl.when(jnp.logical_not(is_odd))
    def _():
        def cross(slot, carry):
            send_forward(slot).wait_recv()

            def rows(tile, carry):
                at = pl.ds(pl.multiple_of(tile * TILE, TILE), TILE)
                docs = cross_in[slot, BLOCK:].astype(F32)
                docs = jnp.where(tile == 0, docs[0:2], docs[2:4])
                mixed, log_sum = attend(chain(cross_in[slot, at]), every, query_documents(docs, tile))
                part_cross_out[slot, at] = mixed
                log_ref[tile] = log_rows(log_sum)
                return carry

            lax.fori_loop(0, BLOCK // TILE, rows, 0)
            part_cross_out[slot, BLOCK:] = pieces(jnp.concatenate([log_ref[0], log_ref[1]], axis=0))
            send_part_cross(slot).start()
            return carry

        lax.fori_loop(0, GROUP, cross, 0)

    @pl.when(x == 0)
    def _():
        lone_rows(False)
        send_part_lone(1).start()

    def merge(head, part, count):
        logs = unpieced(part[count * SUB : count * SUB + 16], count)
        for a in range(count):
            at = slice(a * SUB, (a + 1) * SUB)
            log_sum = rows_to_column(logs[a : a + 1], eye)
            old = max_ref[head, at]
            new = jnp.maximum(old, log_sum)
            keep = jnp.exp2(old - new)
            add = jnp.exp2(log_sum - new)
            acc_ref[head, at] = acc_ref[head, at] * keep + part[at].astype(F32) * add
            sum_ref[head, at] = sum_ref[head, at] * keep + add
            max_ref[head, at] = new

    def part_in_arrival(head):
        return pltpu.make_async_remote_copy(
            src_ref=part_in_out.at[head], dst_ref=part_in.at[head],
            send_sem=pi_send.at[head], recv_sem=pi_recv.at[head],
            device_id={"ctx": base + head}, device_id_type=MESH,
        )

    def part_cross_arrival(head):
        return pltpu.make_async_remote_copy(
            src_ref=part_cross_out.at[head], dst_ref=part_cross.at[head],
            send_sem=pc_send.at[head], recv_sem=pc_recv.at[head],
            device_id={"ctx": base - GROUP + head}, device_id_type=MESH,
        )

    def part_lone_arrival(which, head):
        return pltpu.make_async_remote_copy(
            src_ref=part_lone_out, dst_ref=part_lone.at[which, head],
            send_sem=pl_send, recv_sem=pl_recv.at[which, head],
            device_id={"ctx": (1 - which) * GROUP + head}, device_id_type=MESH,
        )

    @pl.when(z > 0)
    def _():
        def body(head, carry):
            @pl.when(head != z)
            def _():
                part_in_arrival(head).wait_recv()

            merge(head, part_in[head], N_SUB)
            return carry

        lax.fori_loop(0, N_HEAD, body, 0)

    @pl.when((x == 2) & (z == 0))
    def _():
        def body(head, carry):
            for which in range(2):
                part_lone_arrival(which, head).wait_recv()
                merge(head, part_lone[which, head], 2)
            return carry

        lax.fori_loop(0, N_HEAD, body, 0)

    @pl.when(is_odd)
    def _():
        def body(head, carry):
            part_cross_arrival(head).wait_recv()
            merge(head, part_cross[head], N_SUB)
            return carry

        lax.fori_loop(0, N_HEAD, body, 0)

    for head in range(N_HEAD):
        out_ref[:, head * HEAD : (head + 1) * HEAD] = (acc_ref[head] / sum_ref[head]).astype(BF16)

    for slot in range(GROUP):
        @pl.when(slot != z)
        def _():
            send_packet(slot).wait_send()

        @pl.when(is_odd)
        def _():
            send_forward(slot).wait_send()

        @pl.when(jnp.logical_not(is_odd))
        def _():
            send_part_cross(slot).wait_send()

        if slot > 0:
            @pl.when(slot != z)
            def _():
                send_part_in(slot).wait_send()

    @pl.when((x == 1) | (x == 2))
    def _():
        send_lone().wait_send()

    @pl.when(x < 2)
    def _():
        send_part_lone(0).wait_send()


def attention(queries, keys, values, vectors, logits, docs):
    part = lambda *shape: pltpu.VMEM(shape, BF16)
    wide = lambda *shape: pltpu.VMEM(shape, F32)
    dma = lambda *shape: pltpu.SemaphoreType.DMA(shape)
    return pl.pallas_call(
        attention_kernel,
        out_shape=jax.ShapeDtypeStruct((BLOCK, N_HEAD * HEAD), BF16),
        in_specs=[pl.BlockSpec(memory_space=pltpu.VMEM)] * 6,
        out_specs=pl.BlockSpec(memory_space=pltpu.VMEM),
        scratch_shapes=[
            part(7, SUB, SUB), wide(BLOCK, N_HEAD), part(N_HEAD, PACKET, HEAD), part(GROUP, PACKET, HEAD),
            part(6, BLOCK, HEAD), part(GROUP, PART, HEAD), part(GROUP, PART, HEAD), part(TILE, HEAD), part(TILE, HEAD),
            part(GROUP, PART, HEAD), part(GROUP, PART, HEAD), part(PART_HALF, HEAD), part(N_HEAD, PART, HEAD),
            part(N_HEAD, PART, HEAD), part(2, N_HEAD, PART_HALF, HEAD), wide(2, 2, SUB),
            wide(N_HEAD, BLOCK, HEAD), wide(N_HEAD, BLOCK, HEAD), wide(N_HEAD, BLOCK, HEAD),
            pltpu.SemaphoreType.DMA, dma(GROUP), dma(GROUP), dma(GROUP), dma(GROUP),
            pltpu.SemaphoreType.DMA, pltpu.SemaphoreType.DMA,
            dma(GROUP), dma(GROUP), dma(GROUP), dma(GROUP), pltpu.SemaphoreType.DMA, dma(2, GROUP),
        ],
        compiler_params=pltpu.CompilerParams(
            collective_id=0, has_side_effects=True, vmem_limit_bytes=48 * 1024 * 1024
        ),
    )(queries, keys, values, vectors, logits, docs)


def on_device(queries, keys, values, vectors, logits, docs, out_weight):
    docs = docs.astype(F32).reshape(N_SUB, SUB)
    attended = attention(queries, keys, values, vectors, logits, docs)
    return lax.psum_scatter(
        jnp.dot(attended, out_weight, preferred_element_type=F32).astype(BF16),
        "head",
        scatter_dimension=0,
        tiled=True,
    )


def solution(mesh):
    return jax.shard_map(
        on_device,
        mesh=mesh,
        in_specs=(
            P("ctx", "head"),
            P("ctx", "head"),
            P("ctx", "head"),
            P("ctx", "head"),
            P("ctx", "head"),
            P("ctx"),
            P("head", None),
        ),
        out_specs=P(("ctx", "head"), None),
        check_vma=False,
    )
```

time: 812 us -> 121 us (0.15)
  the two profiles are of different devices: /device:TPU:5 before, /device:TPU:0 now
where the time goes in v1:
time: 121 us
  Pallas kernels  53.2 us (44%)
  waiting for transfers between devices  42.1 us (35%)
  between operations  13.4 us (11%)
  matrix products  6.48 us (5%)
  local copies, waits for them, and re-layouts  5 us (4%)
    pallas_call x1, Pallas kernels, attention(): pl.pallas_call(attention_kernel, out_shape=jax.ShapeDtypeStruct((BLOCK, N...  53.2 us
    reduce_scatter x1, waiting for transfers between devices, on_device(): lax.psum_scatter(jnp.dot(attended, out_weight, preferred_element_type=F32...  42.1 us
    dot_general x1, matrix products, on_device(): jnp.dot(attended, out_weight, preferred_element_type=F32).astype(BF16)  6.48 us
    unnamed x9, local copies, waits for them, and re-layouts  5 us
  transfers between devices with their start and end apart: 1, of which 1 were waited for; matrix products, arithmetic and copies ran while one was open for 0% of the time, Pallas kernels for 0%

profile of v1, /device:TPU:0, one launch (start us, length us, event | category | flops | bytes accessed | tf_op | source)
XLA Modules:
  0.0 120.9 jit_solution(12338173507580766517)
XLA Ops:
  6.5 0.0 reduce-scatter.2.cloned.1.call-start
  6.5 0.7 convert_bitcast_fusion.doc_ref
  7.2 0.8 copy.8.logit_ref
  8.1 0.0 copy-start
  8.1 1.0 copy-done
  9.1 0.0 copy-start.1
  9.1 1.0 copy-done.1
  10.2 0.0 copy-start.2
  10.2 1.0 copy-done.2
  11.2 0.0 copy-start.3
  11.2 1.0 copy-done.3
  12.2 53.2 %shard_map.73 = bf16[512,512]{1,0:T(8,128)(2,1)S(1)} custom-call(bf16[512,512]{1,0:T(8,128)(2,1)S(1)} %copy-done, bf16[512,512]{1,0:T(8,128)(2,1)S(1)} %copy-done.1, bf16[512,512]{1,0:T(8,128)(2,1)S(1)} %copy-done.2, bf16[512,512]{1,0:T(8,128)(2,1)S(1)} %copy-done.3, f32[512,4]{1,0:T(8,128)S(1)} %copy.8.logit_ref, f32[4,128]{1,0:T(4,128)S(1)} %convert_bitcast_fusion.doc_ref), custom_call_target="tpu_custom_call" | custom-call | tf_op jit(solution)/shard_map/pallas_call | solution.py:518
  65.4 6.5 %convolution_convert_fusion = bf16[512,4096]{1,0:T(8,128)(2,1)} fusion(bf16[512,512]{1,0:T(8,128)(2,1)S(1)} %shard_map.73, bf16[512,4096]{1,0:T(8,128)(2,1)} %param.13), kind=kOutput, calls=%fused_computation | convolution fusion | flops 2149580800 | bytes 8912896 | tf_op jit(solution)/shard_map/dot_general | solution.py:543
  71.9 0.0 reduce-scatter.2.cloned.1.call-update
  71.9 42.1 %reduce-scatter.2.cloned.1.call-done = bf16[64,4096]{1,0:T(8,128)(2,1)} async-done(((bf16[512,4096]{1,0:T(8,128)(2,1)}), bf16[64,4096]{1,0:T(8,128)(2,1)}) %reduce-scatter.2.cloned.1.call-update) | async-done | bytes 524304 | tf_op jit(solution)/shard_map/reduce_scatter | solution.py:542
Async XLA Ops:
  6.5 107.5 %reduce-scatter.2.cloned.1.call-start = ((), (), s32[]{:S(2)}) async-start(), calls=%async_computation.1 | async-start | bytes 4718592 | tf_op jit(solution)/shard_map/reduce_scatter | solution.py:542
  8.1 1.0 copy-start
  9.1 1.0 copy-start.1
  10.2 1.0 copy-start.2
  11.2 1.0 copy-start.3
Sparse Core Ops, SparseCore 0:
  72.1 41.9 reduce-scatter.1

commit v2 on v1

--- a/solution.py
+++ b/solution.py
@@ -1,4 +1,3 @@
-import functools
 import math
 
 import jax
@@ -19,6 +18,10 @@
 N_HEAD = 4
 GROUP = 4
 TILE = 256
+COLS = 512
+N_COLS = 8
+ROWS = 64
+MODEL = 4096
 NEG = -1e30
 UNIT = math.log2(math.e) / math.sqrt(HEAD)
 
@@ -69,13 +72,15 @@
     return row, col
 
 
-def attention_kernel(
-    q_ref, k_ref, v_ref, u_ref, logit_ref, doc_ref, out_ref,
-    level_ref, beta_ref, packet_out, packet_in, turned_ref, forward_ref, cross_in, lone_in, lone_out,
+def layer_kernel(
+    q_hbm, k_hbm, v_hbm, u_hbm, logit_ref, doc_ref, w_hbm, out_ref,
+    q_ref, k_ref, v_ref, u_ref, w_ref, level_ref, beta_ref, packet_out, packet_in, turned_ref, forward_ref, cross_in, lone_in, lone_out,
     part_in_out, part_cross_out, part_lone_out, part_in, part_cross, part_lone, log_ref,
     acc_ref, max_ref, sum_ref,
-    own_sem, pk_send, pk_recv, xf_send, xf_recv, lone_send, lone_recv,
+    att_ref, mine_ref, pair_out, pair_in, far_out, far_in, relay_out, relay_in, near_out, near_in,
+    load_sem, w_sem, own_sem, pk_send, pk_recv, xf_send, xf_recv, lone_send, lone_recv,
     pi_send, pi_recv, pc_send, pc_recv, pl_send, pl_recv,
+    pair_send, pair_recv, far_send, far_recv, relay_send, relay_recv, near_send, near_recv,
 ):
     me = lax.axis_index("ctx")
     n_ctx = lax.axis_size("ctx")
@@ -83,13 +88,35 @@
     z = lax.rem(me, GROUP)
     base = x * GROUP
 
+    here = lax.axis_index("head")
+    y = here // 2
+    core = lax.rem(here, 2)
+
     barrier = pltpu.get_barrier_semaphore()
+    others = [y * 2 + 1 - core] + [lax.rem(y + step, 4) * 2 + core for step in (1, 3)]
+    for other in others:
+        pl.semaphore_signal(barrier, inc=1, device_id={"head": other}, device_id_type=MESH)
 
     def greet(step, carry):
         pl.semaphore_signal(barrier, inc=1, device_id={"ctx": lax.rem(me + step, n_ctx)}, device_id_type=MESH)
         return carry
 
     lax.fori_loop(1, n_ctx, greet, 0)
+
+    def load(index, head):
+        source = (q_hbm, k_hbm, v_hbm, u_hbm)[index]
+        target = (q_ref, k_ref, v_ref, u_ref)[index]
+        lanes = pl.ds(pl.multiple_of(head * HEAD, HEAD), HEAD)
+        return pltpu.make_async_copy(source.at[:, lanes], target.at[head], load_sem.at[index, head])
+
+    def start_loads(turn, carry):
+        for index in range(4):
+            load(index, lax.rem(z + 1 + turn, N_HEAD)).start()
+        return carry
+
+    lax.fori_loop(0, N_HEAD, start_loads, 0)
+    weight_load = pltpu.make_async_copy(w_hbm, w_ref, w_sem)
+    weight_load.start()
 
     row, col = identity_masks()
     for level in range(7):
@@ -106,25 +133,25 @@
 
     def head_step(turn, carry):
         head = lax.rem(z + 1 + turn, N_HEAD)
-        lanes = pl.ds(pl.multiple_of(head * HEAD, HEAD), HEAD)
         row, col = identity_masks()
         eye = row == col
         upper = col > row
         lower = col < row
         causal = col <= row
         one = jnp.where(eye, 1.0, 0.0)
-        lane4 = lax.broadcasted_iota(jnp.int32, (BLOCK, N_HEAD), 1)
-        beta = jnp.sum(jnp.where(lane4 == head, beta_ref[...], 0.0), axis=1, keepdims=True)
+        for index in range(4):
+            load(index, head).wait()
+        beta = beta_ref[pl.ds(head, 1), :]
         subs = range(N_SUB)
         at = [slice(a * SUB, (a + 1) * SUB) for a in subs]
-        q = [q_ref[at[a], lanes] for a in subs]
-        k = [k_ref[at[a], lanes] for a in subs]
-        v = [v_ref[at[a], lanes] for a in subs]
-        u = [u_ref[at[a], lanes] for a in subs]
+        q = [q_ref[head, at[a]] for a in subs]
+        k = [k_ref[head, at[a]] for a in subs]
+        v = [v_ref[head, at[a]] for a in subs]
+        u = [u_ref[head, at[a]] for a in subs]
         tau, tau_row, lt, low_t, lt_low, skew_t, qk, skew, aq = [], [], [], [], [], [], [], [], []
         for a in subs:
             wide = u[a].astype(F32)
-            tau.append(beta[at[a]] / (jnp.sum(wide * wide, axis=1, keepdims=True) + 1e-6))
+            tau.append(rows_to_column(beta[:, at[a]], eye) / (jnp.sum(wide * wide, axis=1, keepdims=True) + 1e-6))
             tau_row.append(column_to_rows(tau[a], eye))
             gram = jnp.where(upper, nt(u[a], u[a]) * tau[a], 0.0)
             high, low = halves(gram)
@@ -191,14 +218,14 @@
         packet_out[head, AT_K + 256 : AT_K + 512] = as_b(jnp.concatenate([keys[2], keys[3]], axis=0))
         packet_out[head, AT_V : AT_V + 512] = jnp.concatenate(v, axis=0)
         packet_out[head, AT_T : AT_T + 128] = as_b(whole)
-        docs = doc_ref[...]
+        docs = doc_ref[...].astype(F32)
         packet_out[head, AT_D : AT_D + 16] = as_b(
             jnp.concatenate([docs, jnp.zeros((16 - N_SUB, SUB), F32)], axis=0)
         )
 
         @pl.when(turn == 0)
         def _():
-            pl.semaphore_wait(barrier, n_ctx - 1)
+            pl.semaphore_wait(barrier, n_ctx - 1 + len(others))
 
         @pl.when(turn < N_HEAD - 1)
         def _():
@@ -481,8 +508,88 @@
 
         lax.fori_loop(0, N_HEAD, body, 0)
 
-    for head in range(N_HEAD):
-        out_ref[:, head * HEAD : (head + 1) * HEAD] = (acc_ref[head] / sum_ref[head]).astype(BF16)
+    for side in range(2):
+        for place, step in enumerate((2, 1, 3, 0)):
+            owner = lax.rem(y + step, 4) * 2 + (1 - core if side == 0 else core)
+            rows = pl.ds(pl.multiple_of(owner * ROWS, ROWS), ROWS)
+            for head in range(N_HEAD):
+                att_ref[side, place * ROWS : (place + 1) * ROWS, head * HEAD : (head + 1) * HEAD] = (
+                    acc_ref[head, rows] / sum_ref[head, rows]
+                ).astype(BF16)
+    weight_load.wait()
+
+    def sided(t):
+        sign = 1 - 2 * lax.rem(t, 2)
+        onward = lax.rem(y + sign + 4, 4) * 2 + core
+        back = lax.rem(y - sign + 4, 4) * 2 + core
+        return onward, back
+
+    def columns(t):
+        return pl.ds(pl.multiple_of((t // 2) * COLS + lax.rem(t, 2) * (MODEL // 2), COLS), COLS)
+
+    def remote(source, target, send_sem, recv_sem, t, other):
+        return pltpu.make_async_remote_copy(
+            src_ref=source.at[t], dst_ref=target.at[t], send_sem=send_sem.at[t], recv_sem=recv_sem.at[t],
+            device_id={"head": other}, device_id_type=MESH,
+        )
+
+    def send_pair(t):
+        return remote(pair_out, pair_in, pair_send, pair_recv, t, others[0])
+
+    def send_far(t):
+        return remote(far_out, far_in, far_send, far_recv, t, sided(t)[0])
+
+    def send_relay(t):
+        return remote(relay_out, relay_in, relay_send, relay_recv, t, sided(t)[0])
+
+    def send_near(t):
+        return remote(near_out, near_in, near_send, near_recv, t, sided(t)[1])
+
+    def project(t, carry):
+        @pl.when(t < N_COLS)
+        def _():
+            weights = w_ref[:, columns(t)]
+            pair_out[t] = nn(att_ref[0], weights).astype(BF16)
+            send_pair(t).start()
+            mine_ref[t] = nn(att_ref[1], weights)
+
+        @pl.when((t >= 1) & (t < N_COLS + 1))
+        def _():
+            p = t - 1
+            send_pair(p).wait_recv()
+            both = mine_ref[p] + pair_in[p].astype(F32)
+            up = lax.rem(p, 2) == 0
+            one, two = both[ROWS : 2 * ROWS], both[2 * ROWS : 3 * ROWS]
+            far_out[p] = both[0:ROWS].astype(BF16)
+            send_far(p).start()
+            near_out[p] = jnp.where(up, two, one).astype(BF16)
+            send_near(p).start()
+            mine_ref[p, 0:ROWS] = jnp.where(up, one, two)
+            mine_ref[p, 3 * ROWS :] = both[3 * ROWS :]
+
+        @pl.when(t >= 3)
+        def _():
+            p = t - 3
+            send_far(p).wait_recv()
+            relay_out[p] = (mine_ref[p, 0:ROWS] + far_in[p].astype(F32)).astype(BF16)
+            send_relay(p).start()
+
+        return carry
+
+    lax.fori_loop(0, N_COLS + 3, project, 0)
+
+    def finish(t, carry):
+        send_near(t).wait_recv()
+        send_relay(t).wait_recv()
+        total = mine_ref[t, 3 * ROWS :] + near_in[t].astype(F32) + relay_in[t].astype(F32)
+        out_ref[:, columns(t)] = total.astype(BF16)
+        send_pair(t).wait_send()
+        send_far(t).wait_send()
+        send_near(t).wait_send()
+        send_relay(t).wait_send()
+        return carry
+
+    lax.fori_loop(0, N_COLS, finish, 0)
 
     for slot in range(GROUP):
         @pl.when(slot != z)
@@ -511,40 +618,40 @@
         send_part_lone(0).wait_send()
 
 
-def attention(queries, keys, values, vectors, logits, docs):
+def layer(queries, keys, values, vectors, logits, docs, out_weight):
     part = lambda *shape: pltpu.VMEM(shape, BF16)
     wide = lambda *shape: pltpu.VMEM(shape, F32)
     dma = lambda *shape: pltpu.SemaphoreType.DMA(shape)
     return pl.pallas_call(
-        attention_kernel,
-        out_shape=jax.ShapeDtypeStruct((BLOCK, N_HEAD * HEAD), BF16),
-        in_specs=[pl.BlockSpec(memory_space=pltpu.VMEM)] * 6,
+        layer_kernel,
+        out_shape=jax.ShapeDtypeStruct((ROWS, MODEL), BF16),
+        in_specs=[pl.BlockSpec(memory_space=pl.ANY)] * 4
+        + [pl.BlockSpec(memory_space=pltpu.VMEM)] * 2
+        + [pl.BlockSpec(memory_space=pl.ANY)],
         out_specs=pl.BlockSpec(memory_space=pltpu.VMEM),
         scratch_shapes=[
-            part(7, SUB, SUB), wide(BLOCK, N_HEAD), part(N_HEAD, PACKET, HEAD), part(GROUP, PACKET, HEAD),
+            *[part(N_HEAD, BLOCK, HEAD)] * 4, part(BLOCK, MODEL),
+            part(7, SUB, SUB), wide(N_HEAD, BLOCK), part(N_HEAD, PACKET, HEAD), part(GROUP, PACKET, HEAD),
             part(6, BLOCK, HEAD), part(GROUP, PART, HEAD), part(GROUP, PART, HEAD), part(TILE, HEAD), part(TILE, HEAD),
             part(GROUP, PART, HEAD), part(GROUP, PART, HEAD), part(PART_HALF, HEAD), part(N_HEAD, PART, HEAD),
             part(N_HEAD, PART, HEAD), part(2, N_HEAD, PART_HALF, HEAD), wide(2, 2, SUB),
             wide(N_HEAD, BLOCK, HEAD), wide(N_HEAD, BLOCK, HEAD), wide(N_HEAD, BLOCK, HEAD),
+            part(2, TILE, BLOCK), wide(N_COLS, TILE, COLS), part(N_COLS, TILE, COLS), part(N_COLS, TILE, COLS),
+            *[part(N_COLS, ROWS, COLS)] * 6,
+            dma(4, N_HEAD), pltpu.SemaphoreType.DMA,
             pltpu.SemaphoreType.DMA, dma(GROUP), dma(GROUP), dma(GROUP), dma(GROUP),
             pltpu.SemaphoreType.DMA, pltpu.SemaphoreType.DMA,
             dma(GROUP), dma(GROUP), dma(GROUP), dma(GROUP), pltpu.SemaphoreType.DMA, dma(2, GROUP),
+            *[dma(N_COLS)] * 8,
         ],
         compiler_params=pltpu.CompilerParams(
-            collective_id=0, has_side_effects=True, vmem_limit_bytes=48 * 1024 * 1024
+            collective_id=0, has_side_effects=True, vmem_limit_bytes=60 * 1024 * 1024
         ),
-    )(queries, keys, values, vectors, logits, docs)
+    )(queries, keys, values, vectors, logits, docs, out_weight)
 
 
 def on_device(queries, keys, values, vectors, logits, docs, out_weight):
-    docs = docs.astype(F32).reshape(N_SUB, SUB)
-    attended = attention(queries, keys, values, vectors, logits, docs)
-    return lax.psum_scatter(
-        jnp.dot(attended, out_weight, preferred_element_type=F32).astype(BF16),
-        "head",
-        scatter_dimension=0,
-        tiled=True,
-    )
+    return layer(queries, keys, values, vectors, logits.T, docs.reshape(N_SUB, SUB), out_weight)
 
 
 def solution(mesh):

time: 121 us -> 86.3 us (0.71)
  the two profiles are of different devices: /device:TPU:0 before, /device:TPU:5 now
where the time goes in v2:
time: 86.3 us; the launch traced here: 86.1 us
  Pallas kernels  84.2 us (98%)
  local copies, waits for them, and re-layouts  1.87 us (2%)
    pallas_call x1, Pallas kernels, layer(): pl.pallas_call(layer_kernel, out_shape=jax.ShapeDtypeStruct((ROWS, MODEL)...  84.2 us
    unnamed x1, local copies, waits for them, and re-layouts  1.87 us

profile of v2, /device:TPU:5, one launch (start us, length us, event | category | flops | bytes accessed | tf_op | source)
XLA Modules:
  0.0 86.1 jit_solution(6926812590427672324)
XLA Ops:
  0.0 84.2 %shard_map.73 = bf16[64,4096]{1,0:T(8,128)(2,1)} custom-call(bf16[512,512]{1,0:T(8,128)(2,1)} %q_hbm.1, bf16[512,512]{1,0:T(8,128)(2,1)} %k_hbm.1, bf16[512,512]{1,0:T(8,128)(2,1)} %v_hbm.1, bf16[512,512]{1,0:T(8,128)(2,1)} %u_hbm.1, f32[4,512]{1,0:T(4,128)} %bitcast.2, s32[4,128]{1,0:T(4,128)} %bitcast.3, bf16[512,4096]{1,0:T(8,128)(2,1)} %w_hbm.1), custom_call_target="tpu_custom_call" | custom-call | tf_op jit(solution)/shard_map/pallas_call | solution.py:625
  84.3 1.9 %copy.9 = bf16[64,4096]{1,0:T(8,128)(2,1)} copy(bf16[64,4096]{1,0:T(8,128)(2,1)} %shard_map.73) | data formatting | bytes 1048576

commit v3 on v2

--- a/solution.py
+++ b/solution.py
@@ -23,10 +23,12 @@
 ROWS = 64
 MODEL = 4096
 NEG = -1e30
+TRIANGLE = (0, 1, 3, 6)
 UNIT = math.log2(math.e) / math.sqrt(HEAD)
 
-AT_Q, AT_K, AT_V, AT_T, AT_D = 0, 512, 1024, 1536, 1664
-PACKET = 1680
+TOGETHER = 2
+AT_Q, AT_T, AT_D = 0, 512, 640
+PACKET = 656
 PART = BLOCK + 16
 PART_HALF = TILE + 16
 
@@ -74,11 +76,11 @@
 
 def layer_kernel(
     q_hbm, k_hbm, v_hbm, u_hbm, logit_ref, doc_ref, w_hbm, out_ref,
-    q_ref, k_ref, v_ref, u_ref, w_ref, level_ref, beta_ref, packet_out, packet_in, turned_ref, forward_ref, cross_in, lone_in, lone_out,
+    q_ref, k_ref, v_ref, u_ref, w_ref, level_ref, beta_ref, packet_out, packet_in, keys_out, keys_in, values_in, score_ref, turned_ref, forward_ref, cross_in, lone_in, lone_out,
     part_in_out, part_cross_out, part_lone_out, part_in, part_cross, part_lone, log_ref,
     acc_ref, max_ref, sum_ref,
     att_ref, mine_ref, pair_out, pair_in, far_out, far_in, relay_out, relay_in, near_out, near_in,
-    load_sem, w_sem, own_sem, pk_send, pk_recv, xf_send, xf_recv, lone_send, lone_recv,
+    load_sem, w_sem, own_sem, pk_send, pk_recv, ks_send, ks_recv, vs_send, vs_recv, xf_send, xf_recv, lone_send, lone_recv,
     pi_send, pi_recv, pc_send, pc_recv, pl_send, pl_recv,
     pair_send, pair_recv, far_send, far_recv, relay_send, relay_recv, near_send, near_recv,
 ):
@@ -124,36 +126,70 @@
         level_ref[level] = jnp.where(hit, 1.0, 0.0).astype(BF16)
     beta_ref[...] = 2.0 * jax.nn.sigmoid(logit_ref[...])
 
-    def send_packet(head):
-        return pltpu.make_async_remote_copy(
-            src_ref=packet_out.at[head], dst_ref=packet_in.at[z],
-            send_sem=pk_send.at[head], recv_sem=pk_recv.at[z],
+    def to_group(source, target, send_sem, recv_sem, head, slot):
+        return pltpu.make_async_remote_copy(
+            src_ref=source.at[head], dst_ref=target.at[slot],
+            send_sem=send_sem.at[head], recv_sem=recv_sem.at[slot],
             device_id={"ctx": base + head}, device_id_type=MESH,
         )
 
+    def send_packet(head, slot):
+        return to_group(packet_out, packet_in, pk_send, pk_recv, head, slot)
+
+    def send_keys(head, slot):
+        return to_group(keys_out, keys_in, ks_send, ks_recv, head, slot)
+
+    def send_values(head, slot):
+        return to_group(v_ref, values_in, vs_send, vs_recv, head, slot)
+
+    def wait_value_load(turn, carry):
+        load(2, lax.rem(z + 1 + turn, N_HEAD)).wait()
+        return carry
+
+    lax.fori_loop(0, N_HEAD, wait_value_load, 0)
+    own_values = pltpu.make_async_copy(v_ref.at[z], values_in.at[z], own_sem.at[0])
+    own_values.start()
+    pl.semaphore_wait(barrier, n_ctx - 1 + len(others))
+
+    def start_values(turn, carry):
+        send_values(lax.rem(z + 1 + turn, N_HEAD), z).start()
+        return carry
+
+    lax.fori_loop(0, N_HEAD - 1, start_values, 0)
+
+    def as_b(value):
+        return value.astype(BF16)
+
+    def product(left, right):
+        left_high, left_low = halves(left)
+        right_high, right_low = halves(right)
+        return nn(left_high, right_high) + nn(left_low, right_high) + nn(left_high, right_low)
+
     def head_step(turn, carry):
-        head = lax.rem(z + 1 + turn, N_HEAD)
+        heads = [lax.rem(z + 1 + turn * TOGETHER + i, N_HEAD) for i in range(TOGETHER)]
         row, col = identity_masks()
         eye = row == col
         upper = col > row
         lower = col < row
         causal = col <= row
         one = jnp.where(eye, 1.0, 0.0)
-        for index in range(4):
-            load(index, head).wait()
-        beta = beta_ref[pl.ds(head, 1), :]
-        subs = range(N_SUB)
-        at = [slice(a * SUB, (a + 1) * SUB) for a in subs]
-        q = [q_ref[head, at[a]] for a in subs]
-        k = [k_ref[head, at[a]] for a in subs]
-        v = [v_ref[head, at[a]] for a in subs]
-        u = [u_ref[head, at[a]] for a in subs]
-        tau, tau_row, lt, low_t, lt_low, skew_t, qk, skew, aq = [], [], [], [], [], [], [], [], []
+        for head in heads:
+            for index in (0, 1, 3):
+                load(index, head).wait()
+        subs = range(N_SUB * TOGETHER)
+        at = [slice(a * SUB, (a + 1) * SUB) for a in range(N_SUB)]
+        each = [(head, at[a]) for head in heads for a in range(N_SUB)]
+        betas = [beta_ref[pl.ds(head, 1), :] for head in heads]
+        beta = [row[:, rows] for row in betas for rows in at]
+        q = [q_ref[head, rows] for head, rows in each]
+        k = [k_ref[head, rows] for head, rows in each]
+        u = [u_ref[head, rows] for head, rows in each]
+        tau_row, lt, lt_low = [], [], []
         for a in subs:
             wide = u[a].astype(F32)
-            tau.append(rows_to_column(beta[:, at[a]], eye) / (jnp.sum(wide * wide, axis=1, keepdims=True) + 1e-6))
-            tau_row.append(column_to_rows(tau[a], eye))
-            gram = jnp.where(upper, nt(u[a], u[a]) * tau[a], 0.0)
+            tau = rows_to_column(beta[a], eye) / (jnp.sum(wide * wide, axis=1, keepdims=True) + 1e-6)
+            tau_row.append(column_to_rows(tau, eye))
+            gram = jnp.where(upper, nt(u[a], u[a]) * tau, 0.0)
             high, low = halves(gram)
             lt.append(high)
             lt_low.append(low)
@@ -188,63 +224,74 @@
             intra.append((nt(q[a], k[a]) - nn(y, skew)) * UNIT)
             turned.append((q[a].astype(F32) - nn(y, u[a])) * UNIT)
 
-        def as_b(value):
-            return value.astype(BF16)
-
         t_b = [as_b(trans[a]) for a in subs]
-        near_10 = nt(as_b(turned[1]), as_b(keys[0]))
-        near_32 = nt(as_b(turned[3]), as_b(keys[2]))
-        turned[1] = nt(as_b(turned[1]), t_b[0])
-        turned[3] = nt(as_b(turned[3]), t_b[2])
-        keys[0] = nn(as_b(keys[0]), t_b[1])
-        keys[2] = nn(as_b(keys[2]), t_b[3])
-
-        def product(left, right):
-            left_high, left_low = halves(left)
-            right_high, right_low = halves(right)
-            return nn(left_high, right_high) + nn(left_low, right_high) + nn(left_high, right_low)
-
-        pair_a = product(trans[0], trans[1])
-        pair_b = product(trans[2], trans[3])
-        late = jnp.concatenate([as_b(turned[2]), as_b(turned[3])], axis=0)
-        early = jnp.concatenate([as_b(keys[0]), as_b(keys[1])], axis=0)
-        far = nt(late, early)
-        late = nt(late, as_b(pair_a))
-        early = nn(early, as_b(pair_b))
-        whole = product(pair_a, pair_b)
-        packet_out[head, AT_Q : AT_Q + 256] = as_b(jnp.concatenate([turned[0], turned[1]], axis=0))
-        packet_out[head, AT_Q + 256 : AT_Q + 512] = as_b(late)
-        packet_out[head, AT_K : AT_K + 256] = as_b(early)
-        packet_out[head, AT_K + 256 : AT_K + 512] = as_b(jnp.concatenate([keys[2], keys[3]], axis=0))
-        packet_out[head, AT_V : AT_V + 512] = jnp.concatenate(v, axis=0)
-        packet_out[head, AT_T : AT_T + 128] = as_b(whole)
+        starts = range(0, N_SUB * TOGETHER, N_SUB)
+        near, late, early, far = {}, {}, {}, {}
+        for c in starts:
+            for a in (c, c + 2):
+                near[a] = nt(as_b(turned[a + 1]), as_b(keys[a]))
+                turned[a + 1] = nt(as_b(turned[a + 1]), t_b[a])
+                keys[a] = nn(as_b(keys[a]), t_b[a + 1])
+        pair = {a: product(trans[a], trans[a + 1]) for c in starts for a in (c, c + 2)}
+        for c in starts:
+            late[c] = jnp.concatenate([as_b(turned[c + 2]), as_b(turned[c + 3])], axis=0)
+            early[c] = jnp.concatenate([as_b(keys[c]), as_b(keys[c + 1])], axis=0)
+        for c in starts:
+            far[c] = nt(late[c], early[c])
+            late[c] = nt(late[c], as_b(pair[c]))
+            early[c] = nn(early[c], as_b(pair[c + 2]))
         docs = doc_ref[...].astype(F32)
-        packet_out[head, AT_D : AT_D + 16] = as_b(
-            jnp.concatenate([docs, jnp.zeros((16 - N_SUB, SUB), F32)], axis=0)
-        )
-
-        @pl.when(turn == 0)
-        def _():
-            pl.semaphore_wait(barrier, n_ctx - 1 + len(others))
-
-        @pl.when(turn < N_HEAD - 1)
-        def _():
-            send_packet(head).start()
-
-        tiles = [
-            [intra[0]],
-            [near_10, intra[1]],
-            [far[:SUB, :SUB], far[:SUB, SUB:], intra[2]],
-            [far[SUB:, :SUB], far[SUB:, SUB:], near_32, intra[3]],
-        ]
-        for a in subs:
+        docs_tail = as_b(jnp.concatenate([docs, jnp.zeros((16 - N_SUB, SUB), F32)], axis=0))
+        for head, c in zip(heads, starts):
+            whole = product(pair[c], pair[c + 2])
+            packet_out[head, AT_Q : AT_Q + 256] = as_b(jnp.concatenate([turned[c], turned[c + 1]], axis=0))
+            packet_out[head, AT_Q + 256 : AT_Q + 512] = as_b(late[c])
+            packet_out[head, AT_T : AT_T + 128] = as_b(whole)
+            packet_out[head, AT_D : AT_D + 16] = docs_tail
+            keys_out[head, 0:256] = as_b(early[c])
+            keys_out[head, 256:512] = as_b(jnp.concatenate([keys[c + 2], keys[c + 3]], axis=0))
+
+            @pl.when(head != z)
+            def _():
+                send_packet(head, z).start()
+
+        for head, c in zip(heads, starts):
+            for a in range(N_SUB):
+                score_ref[head, TRIANGLE[a] + a] = intra[c + a]
+            score_ref[head, 1] = near[c]
+            score_ref[head, 8] = near[c + 2]
+            for a in (2, 3):
+                for b in (0, 1):
+                    score_ref[head, TRIANGLE[a] + b] = far[c][(a - 2) * SUB : (a - 1) * SUB, b * SUB : (b + 1) * SUB]
+        return carry
+
+    lax.fori_loop(0, N_HEAD // TOGETHER, head_step, 0)
+
+    own_packet = pltpu.make_async_copy(packet_out.at[z], packet_in.at[z], own_sem.at[1])
+    own_packet.start()
+    own_keys = pltpu.make_async_copy(keys_out.at[z], keys_in.at[z], own_sem.at[2])
+    own_keys.start()
+
+    def start_keys(turn, carry):
+        send_keys(lax.rem(z + 1 + turn, N_HEAD), z).start()
+        return carry
+
+    lax.fori_loop(0, N_HEAD - 1, start_keys, 0)
+
+    def own_attention(head, carry):
+        row, col = identity_masks()
+        eye = row == col
+        causal = col <= row
+        docs = doc_ref[...].astype(F32)
+        for a in range(N_SUB):
+            rows = slice(a * SUB, (a + 1) * SUB)
             mine = rows_to_column(docs[a : a + 1], eye)
             scores = []
             for b in range(a + 1):
                 allowed = mine == docs[b : b + 1]
                 if b == a:
                     allowed = allowed & causal
-                scores.append(jnp.where(allowed, tiles[a][b], NEG))
+                scores.append(jnp.where(allowed, score_ref[head, TRIANGLE[a] + b], NEG))
             top = scores[0]
             for score in scores[1:]:
                 top = jnp.maximum(top, score)
@@ -255,28 +302,18 @@
                 total = total + weight
             total = jnp.sum(total, axis=1, keepdims=True)
             joined = jnp.concatenate([as_b(weight) for weight in weights], axis=1)
-            acc_ref[head, at[a]] = nn(joined, jnp.concatenate(v[: a + 1], axis=0))
-            max_ref[head, at[a]] = jnp.broadcast_to(top, (SUB, HEAD))
-            sum_ref[head, at[a]] = jnp.broadcast_to(total, (SUB, HEAD))
-        return carry
-
-    lax.fori_loop(0, N_HEAD, head_step, 0)
-
-    own = pltpu.make_async_copy(packet_out.at[z], packet_in.at[z], own_sem)
-    own.start()
-    own.wait()
-
-    def packet_arrival(slot):
-        return pltpu.make_async_remote_copy(
-            src_ref=packet_out.at[slot], dst_ref=packet_in.at[slot],
-            send_sem=pk_send.at[slot], recv_sem=pk_recv.at[slot],
-            device_id={"ctx": base + slot}, device_id_type=MESH,
-        )
-
+            acc_ref[head, rows] = nn(joined, v_ref[head, 0 : (a + 1) * SUB])
+            max_ref[head, rows] = jnp.broadcast_to(top, (SUB, HEAD))
+            sum_ref[head, rows] = jnp.broadcast_to(total, (SUB, HEAD))
+        return carry
+
+    lax.fori_loop(0, N_HEAD, own_attention, 0)
+
+    own_packet.wait()
     for slot in range(GROUP):
         @pl.when(slot != z)
         def _():
-            packet_arrival(slot).wait_recv()
+            send_packet(slot, slot).wait_recv()
 
     def transition(slot):
         return packet_in[slot, AT_T : AT_T + 128]
@@ -318,6 +355,14 @@
     row, col = identity_masks()
     eye = row == col
 
+    own_values.wait()
+    own_keys.wait()
+    for slot in range(GROUP):
+        @pl.when(slot != z)
+        def _():
+            send_values(slot, slot).wait_recv()
+            send_keys(slot, slot).wait_recv()
+
     def key_documents(slot):
         docs = packet_in[slot, AT_D : AT_D + 16].astype(F32)
         return [docs[a : a + 1] for a in range(N_SUB)]
@@ -325,7 +370,7 @@
     def attend(turned, slots, query_docs):
         scores = []
         for value, slot in zip(turned, slots):
-            raw = nt(value, packet_in[slot, AT_K : AT_K + BLOCK])
+            raw = nt(value, keys_in[slot])
             for a, docs in enumerate(key_documents(slot)):
                 scores.append(jnp.where(query_docs == docs, raw[:, a * SUB : (a + 1) * SUB], NEG))
         top = scores[0]
@@ -339,7 +384,7 @@
             for weight in weights:
                 total = weight if total is None else total + weight
             joined = jnp.concatenate([weight.astype(BF16) for weight in weights], axis=1)
-            term = nn(joined, packet_in[slot, AT_V : AT_V + BLOCK])
+            term = nn(joined, values_in[slot])
             mixed = term if mixed is None else mixed + term
         total = jnp.sum(total, axis=1, keepdims=True)
         return (mixed / total).astype(BF16), top + jnp.log2(total)
@@ -594,7 +639,9 @@
     for slot in range(GROUP):
         @pl.when(slot != z)
         def _():
-            send_packet(slot).wait_send()
+            send_packet(slot, z).wait_send()
+            send_keys(slot, z).wait_send()
+            send_values(slot, z).wait_send()
 
         @pl.when(is_odd)
         def _():
@@ -632,6 +679,7 @@
         scratch_shapes=[
             *[part(N_HEAD, BLOCK, HEAD)] * 4, part(BLOCK, MODEL),
             part(7, SUB, SUB), wide(N_HEAD, BLOCK), part(N_HEAD, PACKET, HEAD), part(GROUP, PACKET, HEAD),
+            part(N_HEAD, BLOCK, HEAD), part(GROUP, BLOCK, HEAD), part(GROUP, BLOCK, HEAD), wide(N_HEAD, 10, SUB, SUB),
             part(6, BLOCK, HEAD), part(GROUP, PART, HEAD), part(GROUP, PART, HEAD), part(TILE, HEAD), part(TILE, HEAD),
             part(GROUP, PART, HEAD), part(GROUP, PART, HEAD), part(PART_HALF, HEAD), part(N_HEAD, PART, HEAD),
             part(N_HEAD, PART, HEAD), part(2, N_HEAD, PART_HALF, HEAD), wide(2, 2, SUB),
@@ -639,7 +687,7 @@
             part(2, TILE, BLOCK), wide(N_COLS, TILE, COLS), part(N_COLS, TILE, COLS), part(N_COLS, TILE, COLS),
             *[part(N_COLS, ROWS, COLS)] * 6,
             dma(4, N_HEAD), pltpu.SemaphoreType.DMA,
-            pltpu.SemaphoreType.DMA, dma(GROUP), dma(GROUP), dma(GROUP), dma(GROUP),
+            dma(3), *[dma(GROUP)] * 6, dma(GROUP), dma(GROUP),
             pltpu.SemaphoreType.DMA, pltpu.SemaphoreType.DMA,
             dma(GROUP), dma(GROUP), dma(GROUP), dma(GROUP), pltpu.SemaphoreType.DMA, dma(2, GROUP),
             *[dma(N_COLS)] * 8,

time: 86.3 us -> 82.2 us (0.952)
  Pallas kernels: 84.2 us -> 80.2 us
    pallas_call x1, Pallas kernels: 84.2 us -> 80.2 us  [layer(): pl.pallas_call(layer_kernel, out_shape=jax.ShapeDtypeStruct((ROWS, MODEL)...]
where the time goes in v3:
time: 82.2 us; the launch traced here: 82 us
  Pallas kernels  80.2 us (98%)
  local copies, waits for them, and re-layouts  1.87 us (2%)
    pallas_call x1, Pallas kernels, layer(): pl.pallas_call(layer_kernel, out_shape=jax.ShapeDtypeStruct((ROWS, MODEL)...  80.2 us
    unnamed x1, local copies, waits for them, and re-layouts  1.87 us

profile of v3, /device:TPU:5, one launch (start us, length us, event | category | flops | bytes accessed | tf_op | source)
XLA Modules:
  0.0 82.0 jit_solution(8246611146646978825)
XLA Ops:
  0.0 80.2 %shard_map.73 = bf16[64,4096]{1,0:T(8,128)(2,1)} custom-call(bf16[512,512]{1,0:T(8,128)(2,1)} %q_hbm.1, bf16[512,512]{1,0:T(8,128)(2,1)} %k_hbm.1, bf16[512,512]{1,0:T(8,128)(2,1)} %v_hbm.1, bf16[512,512]{1,0:T(8,128)(2,1)} %u_hbm.1, f32[4,512]{1,0:T(4,128)} %bitcast.2, s32[4,128]{1,0:T(4,128)} %bitcast.3, bf16[512,4096]{1,0:T(8,128)(2,1)} %w_hbm.1), custom_call_target="tpu_custom_call" | custom-call | tf_op jit(solution)/shard_map/pallas_call | solution.py:672
  80.2 1.9 %copy.9 = bf16[64,4096]{1,0:T(8,128)(2,1)} copy(bf16[64,4096]{1,0:T(8,128)(2,1)} %shard_map.73) | data formatting | bytes 1048576

commit v4 on v3

v4 whole, which is shorter than its diff:
```python
import math

import jax
import jax.numpy as jnp
from jax import lax
from jax.experimental import pallas as pl
from jax.experimental.pallas import tpu as pltpu
from jax.sharding import PartitionSpec as P

MESH = pl.DeviceIdType.MESH
F32 = jnp.float32
BF16 = jnp.bfloat16

HEAD = 128
BLOCK = 512
SUB = 128
N_SUB = 4
N_HEAD = 4
GROUP = 4
TILE = 256
COLS = 1024
N_COLS = 8
ROWS = 32
OWNERS = 8
MODEL = 4096
NEG = -1e30
TRIANGLE = (0, 1, 3, 6)
UNIT = math.log2(math.e) / math.sqrt(HEAD)

TOGETHER = 2
PAIRED = 2
AT_Q, AT_T, AT_D = 0, 512, 640
PACKET = 656
FORWARD = 16 + BLOCK
PART = TILE + 16


def nn(a, b):
    return lax.dot_general(a, b, (((1,), (0,)), ((), ())), preferred_element_type=F32)


def nt(a, b):
    return lax.dot_general(a, b, (((1,), (1,)), ((), ())), preferred_element_type=F32)


def halves(a):
    high = a.astype(BF16)
    return high, (a - high.astype(F32)).astype(BF16)


def rows_to_column(row, eye):
    return jnp.sum(jnp.where(eye, row, 0.0), axis=1, keepdims=True)


def column_to_rows(column, eye):
    return jnp.sum(jnp.where(eye, column, 0.0), axis=0, keepdims=True)


def pieces(rows):
    high = rows.astype(BF16).astype(F32)
    rest = rows - high
    middle = rest.astype(BF16).astype(F32)
    low = rest - middle
    pad = jnp.zeros((16 - 3 * rows.shape[0], rows.shape[1]), F32)
    return jnp.concatenate([high, middle, low, pad], axis=0).astype(BF16)


def unpieced(tail, count):
    tail = tail.astype(F32)
    return tail[:count] + tail[count : 2 * count] + tail[2 * count : 3 * count]


def identity_masks():
    row = lax.broadcasted_iota(jnp.int32, (SUB, SUB), 0)
    col = lax.broadcasted_iota(jnp.int32, (SUB, SUB), 1)
    return row, col


def layer_kernel(
    q_hbm, k_hbm, v_hbm, u_hbm, logit_ref, doc_ref, w_hbm, out_ref,
    q_ref, k_ref, v_ref, u_ref, w_ref, level_ref, beta_ref, packet_out, packet_in, keys_out, keys_in, values_in, score_ref,
    z_ref, y_ref, step_ref, near_ref, far_ref, pair_ref, turned_ref, early_ref, end_ref, forward_ref, cross_in, lone_in, lone_out,
    part_in_out, part_cross_out, part_lone_out, part_in, part_cross, part_lone,
    acc_ref, max_ref, sum_ref,
    att_ref, mine_ref, pair_out, pair_in, far_out, far_in, relay_out, relay_in, near_out, near_in,
    load_sem, w_sem, own_sem, pk_send, pk_recv, ks_send, ks_recv, vs_send, vs_recv, xf_send, xf_recv, lone_send, lone_recv,
    pi_send, pi_recv, pc_send, pc_recv, pl_send, pl_recv,
    pair_send, pair_recv, far_send, far_recv, relay_send, relay_recv, near_send, near_recv,
):
    me = lax.axis_index("ctx")
    n_ctx = lax.axis_size("ctx")
    x = me // GROUP
    z = lax.rem(me, GROUP)
    base = x * GROUP

    here = lax.axis_index("head")
    y = here // 2
    core = lax.rem(here, 2)

    barrier = pltpu.get_barrier_semaphore()
    others = [y * 2 + 1 - core] + [lax.rem(y + step, 4) * 2 + core for step in (1, 3)]
    for other in others:
        pl.semaphore_signal(barrier, inc=1, device_id={"head": other}, device_id_type=MESH)

    def greet(step, carry):
        pl.semaphore_signal(barrier, inc=1, device_id={"ctx": lax.rem(me + step, n_ctx)}, device_id_type=MESH)
        return carry

    lax.fori_loop(1, n_ctx, greet, 0)

    def load(index, head):
        source = (q_hbm, k_hbm, v_hbm, u_hbm)[index]
        target = (q_ref, k_ref, v_ref, u_ref)[index]
        lanes = pl.ds(pl.multiple_of(head * HEAD, HEAD), HEAD)
        return pltpu.make_async_copy(source.at[:, lanes], target.at[head], load_sem.at[index, head])

    def start_loads(turn, carry):
        for index in range(4):
            load(index, lax.rem(z + 1 + turn, N_HEAD)).start()
        return carry

    lax.fori_loop(0, N_HEAD, start_loads, 0)
    weight_load = pltpu.make_async_copy(w_hbm, w_ref, w_sem)
    weight_load.start()

    row, col = identity_masks()
    for level in range(7):
        hit = ((row >> level) + 1 == (col >> level)) & (((row >> level) & 1) == 0)
        level_ref[level] = jnp.where(hit, 1.0, 0.0).astype(BF16)
    beta_ref[...] = 2.0 * jax.nn.sigmoid(logit_ref[...])

    def to_group(source, target, send_sem, recv_sem, head, slot):
        return pltpu.make_async_remote_copy(
            src_ref=source.at[head], dst_ref=target.at[slot],
            send_sem=send_sem.at[head], recv_sem=recv_sem.at[slot],
            device_id={"ctx": base + head}, device_id_type=MESH,
        )

    def send_packet(head, slot):
        return to_group(packet_out, packet_in, pk_send, pk_recv, head, slot)

    def send_keys(head, slot):
        return to_group(keys_out, keys_in, ks_send, ks_recv, head, slot)

    def send_values(head, slot):
        return to_group(v_ref, values_in, vs_send, vs_recv, head, slot)

    def wait_value_load(turn, carry):
        load(2, lax.rem(z + 1 + turn, N_HEAD)).wait()
        return carry

    lax.fori_loop(0, N_HEAD, wait_value_load, 0)
    own_values = pltpu.make_async_copy(v_ref.at[z], values_in.at[z], own_sem.at[0])
    own_values.start()
    pl.semaphore_wait(barrier, n_ctx - 1 + len(others))

    def start_values(turn, carry):
        send_values(lax.rem(z + 1 + turn, N_HEAD), z).start()
        return carry

    lax.fori_loop(0, N_HEAD - 1, start_values, 0)

    def as_b(value):
        return value.astype(BF16)

    def beside(*parts):
        return jnp.concatenate(parts, axis=1)

    def below(*parts):
        return jnp.concatenate(parts, axis=0)

    def product(left, right):
        left_high, left_low = halves(left)
        right_high, right_low = halves(right)
        return nn(beside(left_high, left_low, left_high), below(right_high, right_high, right_low))

    subs = range(N_SUB * TOGETHER)
    starts = range(0, N_SUB * TOGETHER, N_SUB)
    sub_rows = [slice(a * SUB, (a + 1) * SUB) for a in range(N_SUB)]

    def heads_of(turn):
        return [lax.rem(z + 1 + turn * TOGETHER + i, N_HEAD) for i in range(TOGETHER)]

    def store_tiles(target, head, first, value):
        for i in range(value.shape[0] // (2 * ROWS)):
            for tile in range(2):
                to = tile * TILE + (first + i) * ROWS
                target[head, to : to + ROWS] = value[(2 * i + tile) * ROWS : (2 * i + tile + 1) * ROWS]

    def query_step(turn, carry):
        heads = heads_of(turn)
        row, col = identity_masks()
        eye = row == col
        upper = col > row
        causal = col <= row
        one = jnp.where(eye, 1.0, 0.0)
        for head in heads:
            for index in (0, 1, 3):
                load(index, head).wait()
        each = [(head, rows) for head in heads for rows in sub_rows]
        betas = [beta_ref[pl.ds(head, 1), :] for head in heads]
        beta = [row[:, rows] for row in betas for rows in sub_rows]
        q = [q_ref[head, rows] for head, rows in each]
        u = [u_ref[head, rows] for head, rows in each]
        tau_row, lt, lt_low, dots = [], [], [], []
        for a in subs:
            wide = u[a].astype(F32)
            tau = rows_to_column(beta[a], eye) / (jnp.sum(wide * wide, axis=1, keepdims=True) + 1e-6)
            tau_row.append(column_to_rows(tau, eye))
            grams = nt(below(u[a], q[a]), u[a])
            dots.append(jnp.where(causal, grams[SUB:], 0.0) * tau_row[a])
            high, low = halves(jnp.where(upper, grams[:SUB] * tau, 0.0))
            lt.append(high)
            lt_low.append(low)
        inverse = []
        for a in subs:
            inverse.append((one - (lt[a] * level_ref[0]).astype(F32)).astype(BF16))
        for level in range(1, 7):
            first = [nn(inverse[a], lt[a] * level_ref[level]).astype(BF16) for a in subs]
            inverse = [
                (inverse[a].astype(F32) - nn(first[a], inverse[a])).astype(BF16) for a in subs
            ]
        residual = []
        for a in subs:
            both = nn(below(lt[a], lt_low[a]), inverse[a])
            residual.append((one - inverse[a].astype(F32) - (both[:SUB] + both[SUB:])).astype(BF16))
        solved = [inverse[a].astype(F32) + nn(inverse[a], residual[a]) for a in subs]
        trans, turned, z_full = [], [], []
        for a in subs:
            high, low = halves(solved[a] * tau_row[a])
            z_full.append(nn(beside(high, low), below(u[a], u[a])))
        for a in subs:
            head, rows = each[a]
            high, low = halves(z_full[a])
            across = u[a].astype(F32).T.astype(BF16)
            trans.append(one - nn(beside(across, across), below(high, low)))
            z_ref[head, rows] = high
        for a in subs:
            head, rows = each[a]
            a_high, a_low = halves(dots[a])
            s_high, s_low = halves(solved[a])
            y = nt(beside(a_high, a_low, a_high), beside(s_high, s_high, s_low)).astype(BF16)
            y_ref[head, rows] = y
            turned.append(as_b((q[a].astype(F32) - nn(y, u[a])) * UNIT))
        for a in subs:
            head, rows = each[a]
            step_ref[head, rows] = as_b(trans[a])
            near_ref[head, rows] = turned[a]
        pair = {}
        for c in starts:
            for a in (c, c + 2):
                turned[a + 1] = as_b(nt(turned[a + 1], as_b(trans[a])))
                pair[a] = product(trans[a], trans[a + 1])
        docs = doc_ref[...].astype(F32)
        docs_tail = as_b(below(docs, jnp.zeros((16 - N_SUB, SUB), F32)))
        for head, c in zip(heads, starts):
            late = below(turned[c + 2], turned[c + 3])
            far_ref[head] = late
            store_tiles(packet_out, head, 0, below(turned[c], turned[c + 1]))
            store_tiles(packet_out, head, OWNERS // 2, as_b(nt(late, as_b(pair[c]))))
            packet_out[head, AT_T : AT_T + 128] = as_b(product(pair[c], pair[c + 2]))
            packet_out[head, AT_D : AT_D + 16] = docs_tail
            pair_ref[head] = as_b(pair[c + 2])

            @pl.when(head != z)
            def _():
                send_packet(head, z).start()

        return carry

    def key_step(turn, carry):
        heads = heads_of(turn)
        row, col = identity_masks()
        upper = col > row
        lower = col < row
        each = [(head, rows) for head in heads for rows in sub_rows]
        q = [q_ref[head, rows] for head, rows in each]
        k = [k_ref[head, rows] for head, rows in each]
        u = [u_ref[head, rows] for head, rows in each]
        keys = []
        for a in subs:
            head, rows = each[a]
            skew_t = jnp.where(upper, nt(k[a], u[a]), 0.0).astype(BF16)
            keys.append(as_b(k[a].astype(F32) - nn(skew_t, z_ref[head, rows])))
        for a in subs:
            head, rows = each[a]
            grams = nt(below(u[a], q[a]), k[a])
            skew = jnp.where(lower, grams[:SUB], 0.0).astype(BF16)
            at = a % N_SUB
            score_ref[head, TRIANGLE[at] + at] = (grams[SUB:] - nn(y_ref[head, rows], skew)) * UNIT
        for head, c in zip(heads, starts):
            for a in (0, 2):
                score_ref[head, TRIANGLE[a + 1] + a] = nt(near_ref[head, sub_rows[a + 1]], keys[c + a])
                keys[c + a] = as_b(nn(keys[c + a], step_ref[head, sub_rows[a + 1]]))
        for head, c in zip(heads, starts):
            early = below(keys[c], keys[c + 1])
            far = nt(far_ref[head], early)
            keys_out[head, 0:256] = as_b(nn(early, pair_ref[head]))
            keys_out[head, 256:512] = below(keys[c + 2], keys[c + 3])
            for a in (2, 3):
                for b in (0, 1):
                    score_ref[head, TRIANGLE[a] + b] = far[(a - 2) * SUB : (a - 1) * SUB, b * SUB : (b + 1) * SUB]

            @pl.when(head != z)
            def _():
                send_keys(head, z).start()

        return carry

    lax.fori_loop(0, N_HEAD // TOGETHER, query_step, 0)
    lax.fori_loop(0, N_HEAD // TOGETHER, key_step, 0)

    own_packet = pltpu.make_async_copy(packet_out.at[z], packet_in.at[z], own_sem.at[1])
    own_packet.start()
    own_keys = pltpu.make_async_copy(keys_out.at[z], keys_in.at[z], own_sem.at[2])
    own_keys.start()

    def own_attention(head, carry):
        row, col = identity_masks()
        eye = row == col
        causal = col <= row
        docs = doc_ref[...].astype(F32)
        for a in range(N_SUB):
            mine = rows_to_column(docs[a : a + 1], eye)
            scores = []
            for b in range(a + 1):
                allowed = mine == docs[b : b + 1]
                if b == a:
                    allowed = allowed & causal
                scores.append(jnp.where(allowed, score_ref[head, TRIANGLE[a] + b], NEG))
            top = scores[0]
            for score in scores[1:]:
                top = jnp.maximum(top, score)
            top = jnp.max(top, axis=1, keepdims=True)
            weights = [jnp.exp2(score - top) for score in scores]
            total = weights[0]
            for weight in weights[1:]:
                total = total + weight
            total = jnp.sum(total, axis=1, keepdims=True)
            joined = jnp.concatenate([as_b(weight) for weight in weights], axis=1)
            store_tiles(acc_ref, head, 2 * a, nn(joined, v_ref[head, 0 : (a + 1) * SUB]))
            store_tiles(max_ref, head, 2 * a, jnp.broadcast_to(top, (SUB, HEAD)))
            store_tiles(sum_ref, head, 2 * a, jnp.broadcast_to(total, (SUB, HEAD)))
        return carry

    own_packet.wait()
    for slot in range(GROUP):
        @pl.when(slot != z)
        def _():
            send_packet(slot, slot).wait_recv()

    def transition(slot):
        return packet_in[slot, AT_T : AT_T + 128]

    def send_forward(slot, tile):
        rows = pl.ds(0, 16 + TILE) if tile == 0 else pl.ds(16 + TILE, TILE)
        return pltpu.make_async_remote_copy(
            src_ref=forward_ref.at[slot, rows], dst_ref=cross_in.at[slot, rows],
            send_sem=xf_send.at[tile, slot], recv_sem=xf_recv.at[tile, slot],
            device_id={"ctx": lax.rem(me + n_ctx - GROUP, n_ctx)}, device_id_type=MESH,
        )

    def send_lone():
        return pltpu.make_async_remote_copy(
            src_ref=lone_out, dst_ref=lone_in,
            send_sem=lone_send, recv_sem=lone_recv,
            device_id={"ctx": lax.rem(me + n_ctx - GROUP, n_ctx)}, device_id_type=MESH,
        )

    @pl.when(x == 2)
    def _():
        lone_out[...] = below(packet_in[0, 0:SUB], packet_in[0, TILE : TILE + SUB])
        send_lone().start()

    is_odd = lax.rem(x, 2) == 1
    trans = [transition(slot) for slot in range(GROUP)]
    pair_low = as_b(nn(trans[0], trans[1]))
    pair_high = as_b(nn(trans[2], trans[3]))
    turned_last = as_b(nt(packet_in[3, 0:BLOCK], trans[2]))
    turned_ref[...] = turned_last
    for slot in range(GROUP):
        forward_ref[slot, 0:16] = packet_in[slot, AT_D : AT_D + 16]
    forward_ref[0, 16:] = packet_in[0, 0:BLOCK]
    forward_ref[1, 16:] = as_b(nt(packet_in[1, 0:BLOCK], trans[0]))
    forward_ref[2, 16:] = as_b(nt(packet_in[2, 0:BLOCK], pair_low))
    forward_ref[3, 16:] = as_b(nt(turned_last, pair_low))

    @pl.when(is_odd)
    def _():
        for slot in range(GROUP):
            send_forward(slot, 0).start()

    lax.fori_loop(0, N_HEAD, own_attention, 0)

    @pl.when(x == 1)
    def _():
        send_lone().wait_recv()
        lone_out[...] = as_b(nt(lone_in[...], as_b(nn(pair_low, pair_high))))
        send_lone().start()

    @pl.when(is_odd)
    def _():
        for slot in range(GROUP):
            send_forward(slot, 1).start()

    row, col = identity_masks()
    eye = row == col

    own_values.wait()
    own_keys.wait()
    for slot in range(GROUP):
        @pl.when(slot != z)
        def _():
            send_values(slot, slot).wait_recv()
            send_keys(slot, slot).wait_recv()

    early_ref[0:BLOCK] = as_b(nn(keys_in[0], trans[1]))
    early_ref[BLOCK:] = keys_in[1]
    end_ref[0 : 2 * BLOCK] = as_b(nn(early_ref[...], pair_high))
    end_ref[2 * BLOCK : 3 * BLOCK] = as_b(nn(keys_in[2], trans[3]))
    end_ref[3 * BLOCK :] = keys_in[3]

    def key_documents(first, last):
        rows = []
        for slot in range(first, last):
            docs = packet_in[slot, AT_D : AT_D + 16].astype(F32)
            rows += [docs[a : a + 1] for a in range(N_SUB)]
        return rows

    def attend(pieces_of_keys, query_docs):
        scores = []
        for value, keys, first, last in pieces_of_keys:
            raw = nt(value, keys)
            for a, docs in enumerate(key_documents(first, last)):
                scores.append(jnp.where(query_docs == docs, raw[:, a * SUB : (a + 1) * SUB], NEG))
        top = scores[0]
        for score in scores[1:]:
            top = jnp.maximum(top, score)
        top = jnp.max(top, axis=1, keepdims=True)
        weights = [jnp.exp2(score - top) for score in scores]
        total = weights[0]
        for weight in weights[1:]:
            total = total + weight
        total = jnp.sum(total, axis=1, keepdims=True)
        mixed = None
        at = 0
        for _, _, first, last in pieces_of_keys:
            count = (last - first) * N_SUB
            joined = jnp.concatenate([as_b(weight) for weight in weights[at : at + count]], axis=1)
            at += count
            values = jnp.concatenate([values_in[slot] for slot in range(first, last)], axis=0)
            term = nn(joined, values)
            mixed = term if mixed is None else mixed + term
        return as_b(mixed / total), top + jnp.log2(total)

    def query_documents(docs, tile):
        columns = [rows_to_column(docs[a : a + 1], eye) for a in range(N_SUB)]
        return jnp.concatenate(
            [
                columns[owner // 2][(2 * (owner % 2) + tile) * ROWS : (2 * (owner % 2) + tile + 1) * ROWS]
                for owner in range(OWNERS)
            ],
            axis=0,
        )

    def log_rows(log_sum):
        return jnp.concatenate(
            [column_to_rows(log_sum[a * SUB : (a + 1) * SUB], eye) for a in range(2)], axis=0
        )

    def send_part_in(slot):
        return pltpu.make_async_remote_copy(
            src_ref=part_in_out.at[slot], dst_ref=part_in.at[z],
            send_sem=pi_send.at[slot], recv_sem=pi_recv.at[z],
            device_id={"ctx": base + slot}, device_id_type=MESH,
        )

    def send_part_lone(which):
        return pltpu.make_async_remote_copy(
            src_ref=part_lone_out, dst_ref=part_lone.at[which, z],
            send_sem=pl_send, recv_sem=pl_recv.at[which, z],
            device_id={"ctx": 2 * GROUP}, device_id_type=MESH,
        )

    def lone_rows():
        mixed, log_sum = attend([(lone_in[...], end_ref[...], 0, GROUP)], jnp.zeros((TILE, 1), F32))
        part_lone_out[0:TILE] = mixed
        part_lone_out[TILE:] = pieces(log_rows(log_sum))
        send_part_lone(1 - x).start()

    @pl.when(x == 1)
    def _():
        lone_rows()

    def send_part_in(slot, tile):
        return pltpu.make_async_remote_copy(
            src_ref=part_in_out.at[tile, slot], dst_ref=part_in.at[tile, z],
            send_sem=pi_send.at[tile, slot], recv_sem=pi_recv.at[tile, z],
            device_id={"ctx": base + slot}, device_id_type=MESH,
        )

    for tile in range(2):
        at = slice(tile * TILE, (tile + 1) * TILE)
        work = {
            1: [(packet_in[1, at], keys_in[0], 0, 1)],
            2: [(packet_in[2, at], early_ref[...], 0, 2)],
            3: [(packet_in[3, at], keys_in[2], 2, 3), (turned_ref[at], early_ref[...], 0, 2)],
        }
        for slot, parts in work.items():
            docs = packet_in[slot, AT_D : AT_D + 16].astype(F32)
            mixed, log_sum = attend(parts, query_documents(docs, tile))
            part_in_out[tile, slot, 0:TILE] = mixed
            part_in_out[tile, slot, TILE:] = pieces(log_rows(log_sum))
        for slot in work:
            @pl.when(slot != z)
            def _():
                send_part_in(slot, tile).start()

            @pl.when(slot == z)
            def _():
                part_in[tile, z] = part_in_out[tile, slot]

    def send_part_cross(slot, tile):
        return pltpu.make_async_remote_copy(
            src_ref=part_cross_out.at[tile, slot], dst_ref=part_cross.at[tile, z],
            send_sem=pc_send.at[tile, slot], recv_sem=pc_recv.at[tile, z],
            device_id={"ctx": lax.rem(base + GROUP + slot, n_ctx)}, device_id_type=MESH,
        )

    def cross(step, tile):
        slots = [step * PAIRED + i for i in range(PAIRED)]
        for slot in slots:
            send_forward(slot, tile).wait_recv()
        for slot in slots:
            docs = cross_in[slot, 0:16].astype(F32)
            value = cross_in[slot, 16 + tile * TILE : 16 + (tile + 1) * TILE]
            mixed, log_sum = attend([(value, end_ref[...], 0, GROUP)], query_documents(docs, tile))
            part_cross_out[tile, slot, 0:TILE] = mixed
            part_cross_out[tile, slot, TILE:] = pieces(log_rows(log_sum))
        for slot in slots:
            send_part_cross(slot, tile).start()

    @pl.when(x == 0)
    def _():
        send_lone().wait_recv()
        lone_rows()

    @pl.when(jnp.logical_not(is_odd))
    def _():
        for tile in range(2):
            def body(step, carry):
                cross(step, tile)
                return carry

            lax.fori_loop(0, GROUP // PAIRED, body, 0)


    def merge(head, at, values, log_row):
        log_sum = rows_to_column(log_row, eye)
        old = max_ref[head, at]
        new = jnp.maximum(old, log_sum)
        keep = jnp.exp2(old - new)
        add = jnp.exp2(log_sum - new)
        acc_ref[head, at] = acc_ref[head, at] * keep + values.astype(F32) * add
        sum_ref[head, at] = sum_ref[head, at] * keep + add
        max_ref[head, at] = new

    def merge_tile(head, tile, part):
        logs = unpieced(part[TILE:], 2)
        for i in range(2):
            at = slice(tile * TILE + i * SUB, tile * TILE + (i + 1) * SUB)
            merge(head, at, part[i * SUB : (i + 1) * SUB], logs[i : i + 1])

    def part_arrival(source, target, send_sem, recv_sem, tile, head, device):
        return pltpu.make_async_remote_copy(
            src_ref=source.at[tile, head], dst_ref=target.at[tile, head],
            send_sem=send_sem.at[tile, head], recv_sem=recv_sem.at[tile, head],
            device_id={"ctx": device}, device_id_type=MESH,
        )

    def part_lone_arrival(which, head):
        return pltpu.make_async_remote_copy(
            src_ref=part_lone_out, dst_ref=part_lone.at[which, head],
            send_sem=pl_send, recv_sem=pl_recv.at[which, head],
            device_id={"ctx": (1 - which) * GROUP + head}, device_id_type=MESH,
        )

    def gather(tile):
        @pl.when(z > 0)
        def _():
            def body(head, carry):
                @pl.when(head != z)
                def _():
                    part_arrival(part_in_out, part_in, pi_send, pi_recv, tile, head, base + head).wait_recv()

                merge_tile(head, tile, part_in[tile, head])
                return carry

            lax.fori_loop(0, N_HEAD, body, 0)

        @pl.when((x == 2) & (z == 0))
        def _():
            def body(head, carry):
                for which in range(2):
                    if tile == 0:
                        part_lone_arrival(which, head).wait_recv()
                    part = part_lone[which, head]
                    logs = unpieced(part[TILE:], 2)
                    at = slice(tile * TILE, tile * TILE + SUB)
                    merge(head, at, part[tile * SUB : (tile + 1) * SUB], logs[tile : tile + 1])
                return carry

            lax.fori_loop(0, N_HEAD, body, 0)

        @pl.when(is_odd)
        def _():
            def body(head, carry):
                part_arrival(
                    part_cross_out, part_cross, pc_send, pc_recv, tile, head, base - GROUP + head
                ).wait_recv()
                merge_tile(head, tile, part_cross[tile, head])
                return carry

            lax.fori_loop(0, N_HEAD, body, 0)

        for side in range(2):
            for place, step in enumerate((2, 1, 3, 0)):
                owner = lax.rem(y + step, 4) * 2 + (1 - core if side == 0 else core)
                rows = pl.ds(pl.multiple_of(tile * TILE + owner * ROWS, ROWS), ROWS)
                to = side * SUB + place * ROWS
                for head in range(N_HEAD):
                    att_ref[tile, to : to + ROWS, head * HEAD : (head + 1) * HEAD] = (
                        acc_ref[head, rows] / sum_ref[head, rows]
                    ).astype(BF16)

    weight_load.wait()
    gather(0)

    def sided(t):
        sign = 1 - 2 * lax.rem(t, 2)
        onward = lax.rem(y + sign + 4, 4) * 2 + core
        back = lax.rem(y - sign + 4, 4) * 2 + core
        return onward, back

    def columns(t):
        return pl.ds(pl.multiple_of((lax.rem(t, 4) // 2) * COLS + lax.rem(t, 2) * (MODEL // 2), COLS), COLS)

    def remote(source, target, send_sem, recv_sem, t, other):
        return pltpu.make_async_remote_copy(
            src_ref=source.at[t], dst_ref=target.at[t], send_sem=send_sem.at[t], recv_sem=recv_sem.at[t],
            device_id={"head": other}, device_id_type=MESH,
        )

    def send_pair(t):
        return remote(pair_out, pair_in, pair_send, pair_recv, t, others[0])

    def send_far(t):
        return remote(far_out, far_in, far_send, far_recv, t, sided(t)[0])

    def send_relay(t):
        return remote(relay_out, relay_in, relay_send, relay_recv, t, sided(t)[0])

    def send_near(t):
        return remote(near_out, near_in, near_send, near_recv, t, sided(t)[1])

    def project(t, carry):
        @pl.when((t >= 1) & (t < N_COLS + 1))
        def _():
            p = t - 1
            send_pair(p).wait_recv()
            both = mine_ref[p] + pair_in[p].astype(F32)
            up = lax.rem(p, 2) == 0
            one, two = both[ROWS : 2 * ROWS], both[2 * ROWS : 3 * ROWS]
            far_out[p] = both[0:ROWS].astype(BF16)
            send_far(p).start()
            near_out[p] = jnp.where(up, two, one).astype(BF16)
            send_near(p).start()
            mine_ref[p, 0:ROWS] = jnp.where(up, one, two)
            mine_ref[p, 3 * ROWS :] = both[3 * ROWS :]

        @pl.when(t == N_COLS // 2)
        def _():
            gather(1)

        @pl.when(t >= 3)
        def _():
            p = t - 3
            send_far(p).wait_recv()
            relay_out[p] = (mine_ref[p, 0:ROWS] + far_in[p].astype(F32)).astype(BF16)
            send_relay(p).start()

        @pl.when(t < N_COLS)
        def _():
            product = nn(att_ref[t // (N_COLS // 2)], w_ref[:, columns(t)])
            pair_out[t] = product[:SUB].astype(BF16)
            send_pair(t).start()
            mine_ref[t] = product[SUB:]

        return carry

    lax.fori_loop(0, N_COLS + 3, project, 0)

    def finish(t, carry):
        send_near(t).wait_recv()
        send_relay(t).wait_recv()
        total = mine_ref[t, 3 * ROWS :] + near_in[t].astype(F32) + relay_in[t].astype(F32)
        rows = pl.ds(pl.multiple_of((t // (N_COLS // 2)) * ROWS, ROWS), ROWS)
        out_ref[rows, columns(t)] = total.astype(BF16)
        send_pair(t).wait_send()
        send_far(t).wait_send()
        send_near(t).wait_send()
        send_relay(t).wait_send()
        return carry

    lax.fori_loop(0, N_COLS, finish, 0)

    for slot in range(GROUP):
        @pl.when(slot != z)
        def _():
            send_packet(slot, z).wait_send()
            send_keys(slot, z).wait_send()
            send_values(slot, z).wait_send()

        for tile in range(2):
            @pl.when(is_odd)
            def _():
                send_forward(slot, tile).wait_send()

            @pl.when(jnp.logical_not(is_odd))
            def _():
                send_part_cross(slot, tile).wait_send()

            if slot > 0:
                @pl.when(slot != z)
                def _():
                    send_part_in(slot, tile).wait_send()

    @pl.when((x == 1) | (x == 2))
    def _():
        send_lone().wait_send()

    @pl.when(x < 2)
    def _():
        send_part_lone(0).wait_send()


def layer(queries, keys, values, vectors, logits, docs, out_weight):
    part = lambda *shape: pltpu.VMEM(shape, BF16)
    wide = lambda *shape: pltpu.VMEM(shape, F32)
    dma = lambda *shape: pltpu.SemaphoreType.DMA(shape)
    return pl.pallas_call(
        layer_kernel,
        out_shape=jax.ShapeDtypeStruct((2 * ROWS, MODEL), BF16),
        in_specs=[pl.BlockSpec(memory_space=pl.ANY)] * 4
        + [pl.BlockSpec(memory_space=pltpu.VMEM)] * 2
        + [pl.BlockSpec(memory_space=pl.ANY)],
        out_specs=pl.BlockSpec(memory_space=pltpu.VMEM),
        scratch_shapes=[
            *[part(N_HEAD, BLOCK, HEAD)] * 4, part(BLOCK, MODEL),
            part(7, SUB, SUB), wide(N_HEAD, BLOCK), part(N_HEAD, PACKET, HEAD), part(GROUP, PACKET, HEAD),
            part(N_HEAD, BLOCK, HEAD), part(GROUP, BLOCK, HEAD), part(GROUP, BLOCK, HEAD), wide(N_HEAD, 10, SUB, SUB),
            *[part(N_HEAD, BLOCK, HEAD)] * 4, part(N_HEAD, TILE, HEAD), part(N_HEAD, SUB, HEAD),
            part(BLOCK, HEAD), part(2 * BLOCK, HEAD), part(4 * BLOCK, HEAD), part(GROUP, FORWARD, HEAD), part(GROUP, FORWARD, HEAD), part(TILE, HEAD), part(TILE, HEAD),
            part(2, GROUP, PART, HEAD), part(2, GROUP, PART, HEAD), part(PART, HEAD), part(2, N_HEAD, PART, HEAD),
            part(2, N_HEAD, PART, HEAD), part(2, N_HEAD, PART, HEAD),
            wide(N_HEAD, BLOCK, HEAD), wide(N_HEAD, BLOCK, HEAD), wide(N_HEAD, BLOCK, HEAD),
            part(2, TILE, BLOCK), wide(N_COLS, SUB, COLS), part(N_COLS, SUB, COLS), part(N_COLS, SUB, COLS),
            *[part(N_COLS, ROWS, COLS)] * 6,
            dma(4, N_HEAD), pltpu.SemaphoreType.DMA,
            dma(3), *[dma(GROUP)] * 6, dma(2, GROUP), dma(2, GROUP),
            pltpu.SemaphoreType.DMA, pltpu.SemaphoreType.DMA,
            *[dma(2, GROUP)] * 4, pltpu.SemaphoreType.DMA, dma(2, GROUP),
            *[dma(N_COLS)] * 8,
        ],
        compiler_params=pltpu.CompilerParams(
            collective_id=0, has_side_effects=True, vmem_limit_bytes=60 * 1024 * 1024
        ),
    )(queries, keys, values, vectors, logits, docs, out_weight)


def on_device(queries, keys, values, vectors, logits, docs, out_weight):
    return layer(queries, keys, values, vectors, logits.T, docs.reshape(N_SUB, SUB), out_weight)


def solution(mesh):
    return jax.shard_map(
        on_device,
        mesh=mesh,
        in_specs=(
            P("ctx", "head"),
            P("ctx", "head"),
            P("ctx", "head"),
            P("ctx", "head"),
            P("ctx", "head"),
            P("ctx"),
            P("head", None),
        ),
        out_specs=P(("ctx", "head"), None),
        check_vma=False,
    )
```

time: 82.2 us -> 72.1 us (0.88)
  the two profiles are of different devices: /device:TPU:5 before, /device:TPU:98 now
where the time goes in v4:
time: 72.1 us; the launch traced here: 71.9 us
  Pallas kernels  70 us (97%)
  local copies, waits for them, and re-layouts  1.87 us (3%)
    pallas_call x1, Pallas kernels, layer(): pl.pallas_call(layer_kernel, out_shape=jax.ShapeDtypeStruct((2 * ROWS, MO...  70 us
    unnamed x1, local copies, waits for them, and re-layouts  1.87 us

profile of v4, /device:TPU:98, one launch (start us, length us, event | category | flops | bytes accessed | tf_op | source)
XLA Modules:
  0.0 71.9 jit_solution(14889800299707615675)
XLA Ops:
  0.0 70.0 %shard_map.73 = bf16[64,4096]{1,0:T(8,128)(2,1)} custom-call(bf16[512,512]{1,0:T(8,128)(2,1)} %q_hbm.1, bf16[512,512]{1,0:T(8,128)(2,1)} %k_hbm.1, bf16[512,512]{1,0:T(8,128)(2,1)} %v_hbm.1, bf16[512,512]{1,0:T(8,128)(2,1)} %u_hbm.1, f32[4,512]{1,0:T(4,128)} %bitcast.2, s32[4,128]{1,0:T(4,128)} %bitcast.3, bf16[512,4096]{1,0:T(8,128)(2,1)} %w_hbm.1), custom_call_target="tpu_custom_call" | custom-call | tf_op jit(solution)/shard_map/pallas_call | solution.py:751
  70.0 1.9 %copy.9 = bf16[64,4096]{1,0:T(8,128)(2,1)} copy(bf16[64,4096]{1,0:T(8,128)(2,1)} %shard_map.73) | data formatting | bytes 1048576

commit v5 on v4

--- a/solution.py
+++ b/solution.py
@@ -499,7 +499,7 @@
             device_id={"ctx": base + slot}, device_id_type=MESH,
         )
 
-    for tile in range(2):
+    def pairs_within(tile):
         at = slice(tile * TILE, (tile + 1) * TILE)
         work = {
             1: [(packet_in[1, at], keys_in[0], 0, 1)],
@@ -540,19 +540,25 @@
         for slot in slots:
             send_part_cross(slot, tile).start()
 
+    def cross_tile(tile):
+        @pl.when(jnp.logical_not(is_odd))
+        def _():
+            def body(step, carry):
+                cross(step, tile)
+                return carry
+
+            lax.fori_loop(0, GROUP // PAIRED, body, 0)
+
+    pairs_within(0)
+    cross_tile(0)
+
     @pl.when(x == 0)
     def _():
         send_lone().wait_recv()
         lone_rows()
 
-    @pl.when(jnp.logical_not(is_odd))
-    def _():
-        for tile in range(2):
-            def body(step, carry):
-                cross(step, tile)
-                return carry
-
-            lax.fori_loop(0, GROUP // PAIRED, body, 0)
+    pairs_within(1)
+    cross_tile(1)
 
 
     def merge(head, at, values, log_row):
@@ -663,42 +669,50 @@
     def send_near(t):
         return remote(near_out, near_in, near_send, near_recv, t, sided(t)[1])
 
+    half = N_COLS // 2
+
+    def stage(t, late, work):
+        p = t - late
+
+        @pl.when((p >= 0) & (p < N_COLS))
+        def _():
+            work(p)
+
+    def pair_up(p):
+        send_pair(p).wait_recv()
+        both = mine_ref[p] + pair_in[p].astype(F32)
+        up = lax.rem(p, 2) == 0
+        one, two = both[ROWS : 2 * ROWS], both[2 * ROWS : 3 * ROWS]
+        far_out[p] = both[0:ROWS].astype(BF16)
+        send_far(p).start()
+        near_out[p] = jnp.where(up, two, one).astype(BF16)
+        send_near(p).start()
+        mine_ref[p, 0:ROWS] = jnp.where(up, one, two)
+        mine_ref[p, 3 * ROWS :] = both[3 * ROWS :]
+
+    def relay(p):
+        send_far(p).wait_recv()
+        relay_out[p] = (mine_ref[p, 0:ROWS] + far_in[p].astype(F32)).astype(BF16)
+        send_relay(p).start()
+
+    def multiply(p):
+        product = nn(att_ref[p // half], w_ref[:, columns(p)])
+        pair_out[p] = product[:SUB].astype(BF16)
+        send_pair(p).start()
+        mine_ref[p] = product[SUB:]
+
     def project(t, carry):
-        @pl.when((t >= 1) & (t < N_COLS + 1))
-        def _():
-            p = t - 1
-            send_pair(p).wait_recv()
-            both = mine_ref[p] + pair_in[p].astype(F32)
-            up = lax.rem(p, 2) == 0
-            one, two = both[ROWS : 2 * ROWS], both[2 * ROWS : 3 * ROWS]
-            far_out[p] = both[0:ROWS].astype(BF16)
-            send_far(p).start()
-            near_out[p] = jnp.where(up, two, one).astype(BF16)
-            send_near(p).start()
-            mine_ref[p, 0:ROWS] = jnp.where(up, one, two)
-            mine_ref[p, 3 * ROWS :] = both[3 * ROWS :]
-
-        @pl.when(t == N_COLS // 2)
+        stage(t, 2, pair_up)
+        stage(t, 5, relay)
+
+        @pl.when(t == half)
         def _():
             gather(1)
 
-        @pl.when(t >= 3)
-        def _():
-            p = t - 3
-            send_far(p).wait_recv()
-            relay_out[p] = (mine_ref[p, 0:ROWS] + far_in[p].astype(F32)).astype(BF16)
-            send_relay(p).start()
-
-        @pl.when(t < N_COLS)
-        def _():
-            product = nn(att_ref[t // (N_COLS // 2)], w_ref[:, columns(t)])
-            pair_out[t] = product[:SUB].astype(BF16)
-            send_pair(t).start()
-            mine_ref[t] = product[SUB:]
-
+        stage(t, 0, multiply)
         return carry
 
-    lax.fori_loop(0, N_COLS + 3, project, 0)
+    lax.fori_loop(0, N_COLS + 5, project, 0)
 
     def finish(t, carry):
         send_near(t).wait_recv()

time: 72.1 us -> 70 us (0.971)
  the two profiles are of different devices: /device:TPU:98 before, /device:TPU:5 now
where the time goes in v5:
time: 70 us; the launch traced here: 69.8 us
  Pallas kernels  67.9 us (97%)
  local copies, waits for them, and re-layouts  1.87 us (3%)
    pallas_call x1, Pallas kernels, layer(): pl.pallas_call(layer_kernel, out_shape=jax.ShapeDtypeStruct((2 * ROWS, MO...  67.9 us
    unnamed x1, local copies, waits for them, and re-layouts  1.87 us

profile of v5, /device:TPU:5, one launch (start us, length us, event | category | flops | bytes accessed | tf_op | source)
XLA Modules:
  0.0 69.8 jit_solution(6388157185761040275)
XLA Ops:
  0.0 67.9 %shard_map.73 = bf16[64,4096]{1,0:T(8,128)(2,1)} custom-call(bf16[512,512]{1,0:T(8,128)(2,1)} %q_hbm.1, bf16[512,512]{1,0:T(8,128)(2,1)} %k_hbm.1, bf16[512,512]{1,0:T(8,128)(2,1)} %v_hbm.1, bf16[512,512]{1,0:T(8,128)(2,1)} %u_hbm.1, f32[4,512]{1,0:T(4,128)} %bitcast.2, s32[4,128]{1,0:T(4,128)} %bitcast.3, bf16[512,4096]{1,0:T(8,128)(2,1)} %w_hbm.1), custom_call_target="tpu_custom_call" | custom-call | tf_op jit(solution)/shard_map/pallas_call | solution.py:765
  67.9 1.9 %copy.9 = bf16[64,4096]{1,0:T(8,128)(2,1)} copy(bf16[64,4096]{1,0:T(8,128)(2,1)} %shard_map.73) | data formatting | bytes 1048576
